TPU v7x, 32 devices: a whole 2x2x4 slice. The times are simulated.
32 devices in a mesh: ctx: 16 (over z, y, x), dp: 2 (over core).
Axes of the slice: x: 2, y: 2, z: 4, core: 2. Of those that a mesh axis runs over, the one named last changes fastest.
Arguments:
- queries: bfloat16 [2048, 2048], P('ctx', 'dp'), may hold values from -192 to 192
- keys: bfloat16 [2048, 128], P('ctx'), may hold values from -32 to 32
- values: bfloat16 [2048, 128], P('ctx'), may hold values from -6 to 6
- out_grads: bfloat16 [2048, 2048], P('ctx', 'dp'), may hold values from -6 to 6
- doc_lengths: int32 [8], replicated, may hold values from 1 to 1152, 2048 in all
Outputs:
- query_grads: bfloat16 [2048, 2048], P('ctx', 'dp')
- key_grads: bfloat16 [2048, 128], P(('ctx', 'dp'))
- value_grads: bfloat16 [2048, 128], P(('ctx', 'dp'))
Inputs may be any that keep to these rules, and one draw needn't show every extreme that they name: `doc_lengths`: document lengths in order of position; they sum to 2048 and the longest document has exactly 1152 tokens.
All inputs are finite; a program needn't handle non-finite values.
Results may differ from a plain program's by a relative error of at most 0.023.
Values may be sent and summed in bfloat16 or wider, within the bound.
No kernel may reach another device: no remote copies, remote signals or barrier semaphores. Data moves between devices by JAX's collectives and lax.ppermute only.
A program may use at most 64 MiB of HBM per device.

v0:
```python
import jax
import jax.numpy as jnp
from jax import lax
from jax.sharding import PartitionSpec as P

masked_value = -1e30


def span_positions(device_ids, tok_rows, ctx_count):
    offsets = jnp.arange(tok_rows, dtype=jnp.int32)[None, :]
    half_rows = tok_rows // 2
    low_pos = device_ids[:, None] * half_rows + offsets
    high_pos = (2 * ctx_count - 1 - device_ids[:, None]) * half_rows + offsets - half_rows
    return jnp.where(offsets < half_rows, low_pos, high_pos)


def doc_ids(positions, doc_lengths):
    doc_ends = jnp.cumsum(doc_lengths)
    return jnp.sum((positions[..., None] >= doc_ends).astype(jnp.int32), axis=-1)


def grouped(members, device_ids, is_valid, tok_rows, ctx_count, doc_lengths):
    block_count = device_ids.shape[0]
    per_step = max(1, min(block_count, 512 // tok_rows))
    padded = -(-block_count // per_step) * per_step
    step_count = padded // per_step
    shaped = [
        member.reshape((step_count, per_step * tok_rows) + member.shape[2:]) for member in members
    ]
    positions = span_positions(jnp.clip(device_ids, 0, ctx_count - 1), tok_rows, ctx_count)
    doc_index = doc_ids(positions, doc_lengths)
    alive_rows = jnp.broadcast_to(is_valid[:, None], positions.shape)
    flat_shape = (step_count, per_step * tok_rows)
    return tuple(shaped) + (
        positions.reshape(flat_shape),
        doc_index.reshape(flat_shape),
        alive_rows.reshape(flat_shape),
    )


def body(queries, keys, values, out_grads, doc_lengths):
    ctx_count = lax.axis_size("ctx")
    ctx_index = lax.axis_index("ctx")
    tok_rows = keys.shape[0]
    head_width = keys.shape[1]
    head_count = queries.shape[1] // head_width
    score_scale = head_width ** (-0.5)
    own_device = jnp.reshape(ctx_index, (1,))
    own_pos = span_positions(own_device, tok_rows, ctx_count)[0]
    own_doc = doc_ids(own_pos, doc_lengths)
    query_heads = queries.reshape(tok_rows, head_count, head_width)
    grad_heads = out_grads.reshape(tok_rows, head_count, head_width)
    keys_all, values_all = (
        lax.all_gather(keys, "ctx", axis=0, tiled=True),
        lax.all_gather(values, "ctx", axis=0, tiled=True),
    )
    key_members = [
        keys_all.reshape(ctx_count, tok_rows, head_width),
        values_all.reshape(ctx_count, tok_rows, head_width),
    ]
    key_devices = jnp.arange(ctx_count, dtype=jnp.int32)
    key_valid = key_devices >= 0
    key_stack = grouped(key_members, key_devices, key_valid, tok_rows, ctx_count, doc_lengths)

    def live_for(key_pos, key_doc, key_alive):
        return (
            key_alive[None, :]
            & (key_pos[None, :] <= own_pos[:, None])
            & (key_doc[None, :] == own_doc[:, None])
        )

    def logits_of(key_block):
        return score_scale * jnp.einsum(
            "thd,kd->htk", query_heads, key_block, preferred_element_type=jnp.float32
        )

    def max_step(state, block_in):
        key_block, value_block, key_pos, key_doc, key_alive = block_in
        live_mask = live_for(key_pos, key_doc, key_alive)
        row_top, row_total = state
        logits = logits_of(key_block)
        new_top = jnp.maximum(
            row_top, jnp.max(jnp.where(live_mask[None], logits, masked_value), axis=2)
        )
        terms = jnp.where(live_mask[None], jnp.exp(logits - new_top[:, :, None]), 0.0)
        return ((new_top, row_total * jnp.exp(row_top - new_top) + jnp.sum(terms, axis=2)), None)

    start_state = (
        jnp.full((head_count, tok_rows), masked_value, jnp.float32),
        jnp.zeros((head_count, tok_rows), jnp.float32),
    )
    (row_top, row_total), _ = lax.scan(max_step, start_state, key_stack)
    row_lse = row_top + jnp.log(row_total)

    def output_step(state, block_in):
        key_block, value_block, key_pos, key_doc, key_alive = block_in
        live_mask = live_for(key_pos, key_doc, key_alive)
        weights_f = jnp.where(
            live_mask[None], jnp.exp(logits_of(key_block) - row_lse[:, :, None]), 0.0
        )
        return (
            state
            + jnp.einsum(
                "htk,kd->htd",
                weights_f.astype(jnp.bfloat16),
                value_block,
                preferred_element_type=jnp.float32,
            ),
            None,
        )

    output, _ = lax.scan(
        output_step, jnp.zeros((head_count, tok_rows, head_width), jnp.float32), key_stack
    )
    delta = jnp.sum(jnp.transpose(grad_heads, (1, 0, 2)).astype(jnp.float32) * output, axis=2)

    def block_terms(key_block, value_block, live_mask):
        weights_f = jnp.where(
            live_mask[None], jnp.exp(logits_of(key_block) - row_lse[:, :, None]), 0.0
        )
        dweights = jnp.einsum(
            "thd,kd->htk", grad_heads, value_block, preferred_element_type=jnp.float32
        )
        dlogits = (weights_f * (dweights - delta[:, :, None])).astype(jnp.bfloat16)
        return (weights_f.astype(jnp.bfloat16), dlogits)

    zero_grads = jnp.zeros((tok_rows, head_width), jnp.float32)
    zero_query = jnp.zeros((tok_rows, head_count, head_width), jnp.float32)

    def query_step(state, block_in):
        key_block, value_block, key_pos, key_doc, key_alive = block_in
        live_mask = live_for(key_pos, key_doc, key_alive)
        weights_low, dlogits = block_terms(key_block, value_block, live_mask)
        return (
            state
            + jnp.einsum("htk,kd->thd", dlogits, key_block, preferred_element_type=jnp.float32),
            None,
        )

    query_sum, _ = lax.scan(query_step, zero_query, key_stack)
    query_grads = (
        (score_scale * query_sum).astype(jnp.bfloat16).reshape(tok_rows, head_count * head_width)
    )
    lse_rows = row_lse.T
    delta_rows = delta.T
    queries_all, grads_all = (
        lax.all_gather(queries, "ctx", axis=0, tiled=True),
        lax.all_gather(out_grads, "ctx", axis=0, tiled=True),
    )
    lse_all, delta_all = (
        lax.all_gather(lse_rows, "ctx", axis=0, tiled=True),
        lax.all_gather(delta_rows, "ctx", axis=0, tiled=True),
    )
    query_members = [
        queries_all.reshape(ctx_count, tok_rows, head_count * head_width),
        grads_all.reshape(ctx_count, tok_rows, head_count * head_width),
        lse_all.reshape(ctx_count, tok_rows, head_count),
        delta_all.reshape(ctx_count, tok_rows, head_count),
    ]
    query_devices = jnp.arange(ctx_count, dtype=jnp.int32)
    query_valid = query_devices >= 0
    query_stack = grouped(
        query_members, query_devices, query_valid, tok_rows, ctx_count, doc_lengths
    )

    def key_step(state, block_in):
        query_block, grad_block, lse_block, delta_block, query_pos, query_doc, query_alive = (
            block_in
        )
        live_mask = (
            query_alive[:, None]
            & (own_pos[None, :] <= query_pos[:, None])
            & (own_doc[None, :] == query_doc[:, None])
        )
        key_sum, value_sum = state
        block_rows = query_block.shape[0]
        query_split = query_block.reshape(block_rows, head_count, head_width)
        grad_split = grad_block.reshape(block_rows, head_count, head_width)
        logits = score_scale * jnp.einsum(
            "rhd,kd->hrk", query_split, keys, preferred_element_type=jnp.float32
        )
        weights_f = jnp.where(live_mask[None], jnp.exp(logits - lse_block.T[:, :, None]), 0.0)
        value_sum = value_sum + jnp.einsum(
            "hrk,rhd->kd",
            weights_f.astype(jnp.bfloat16),
            grad_split,
            preferred_element_type=jnp.float32,
        )
        dweights = jnp.einsum("rhd,kd->hrk", grad_split, values, preferred_element_type=jnp.float32)
        dlogits = (weights_f * (dweights - delta_block.T[:, :, None])).astype(jnp.bfloat16)
        key_sum = key_sum + jnp.einsum(
            "hrk,rhd->kd", dlogits, query_split, preferred_element_type=jnp.float32
        )
        return ((key_sum, value_sum), None)

    (key_part, value_part), _ = lax.scan(key_step, (zero_grads, zero_grads), query_stack)
    key_total, value_total = (
        lax.psum_scatter(
            (score_scale * key_part).astype(jnp.bfloat16), "dp", scatter_dimension=0, tiled=True
        ).astype(jnp.float32),
        lax.psum_scatter(
            value_part.astype(jnp.bfloat16), "dp", scatter_dimension=0, tiled=True
        ).astype(jnp.float32),
    )
    return (query_grads, key_total.astype(jnp.bfloat16), value_total.astype(jnp.bfloat16))


def solution(mesh):
    return jax.shard_map(
        body,
        mesh=mesh,
        in_specs=(P("ctx", "dp"), P("ctx", None), P("ctx", None), P("ctx", "dp"), P()),
        out_specs=(P("ctx", "dp"), P(("ctx", "dp"), None), P(("ctx", "dp"), None)),
        check_vma=False,
    )
```

profile of v0, /device:TPU:0, one launch (start us, length us, event | category | flops | bytes accessed | tf_op | source)
XLA Modules:
  0.0 267.3 jit_solution(8799430900253228460)
XLA Ops:
  11.2 47.0 %all_gather.18 = bf16[2048,128]{1,0:T(8,128)(2,1)S(1)} all-gather(bf16[128,128]{1,0:T(8,128)(2,1)} %param.14), channel_id=1, replica_groups=mesh['ctx'=16,'dp'=2] {'ctx'}, dimensions={0}, use_global_device_ids=true | all-gather | bytes 557056 | tf_op jit(solution)/shard_map/all_gather | solution.py:54
  58.3 4.8 %while.52 = (s32[]{:T(128)}, f32[8,128]{1,0:T(8,128)S(1)}, f32[8,128]{1,0:T(8,128)S(1)}, s32[4,512]{1,0:T(4,128)S(1)}, s32[4,512]{1,0:T(4,128)S(1)}, /*index=5*/...) while((s32[]{:T(128)}, f32[8,128]{1,0:T(8,128)S(1)}, ...), condition=%wide.region_6.7_spmd.clone, body=%wide.region_3.6_spmd.clone.sunk | while | flops 138090112 | bytes 4851352 | solution.py:92
  64.2 41.9 %all_gather.19 = bf16[2048,128]{1,0:T(8,128)(2,1)S(1)} all-gather(bf16[128,128]{1,0:T(8,128)(2,1)S(1)} %copy-done), channel_id=1, replica_groups=mesh['ctx'=16,'dp'=2] {'ctx'}, dimensions={0}, use_global_device_ids=true | all-gather | bytes 557056 | tf_op jit(solution)/shard_map/all_gather | solution.py:55
  106.2 5.2 %while.53 = (s32[]{:T(128)}, f32[8,128,128]{2,1,0:T(8,128)S(1)}, s32[4,512]{1,0:T(4,128)S(1)}, s32[4,512]{1,0:T(4,128)S(1)}, s32[128]{0:T(128)S(1)}, /*index=5*/...) while((s32[]{:T(128)}, f32[8,128,128]{2,1,0:T(8,128)S(1)}, ...), condition=%wide.region_8.9_spmd.clone, body=%wide.region_7.8_spmd.clone.sunk | while | flops 270992000 | bytes 1723546 | solution.py:112
  112.4 38.1 %all_gather.21 = f32[2048,8]{0,1:T(8,128)S(1)} all-gather(f32[128,8]{0,1:T(8,128)S(1)} %bitcast.288), channel_id=1, replica_groups=mesh['ctx'=16,'dp'=2] {'ctx'}, dimensions={0}, use_global_device_ids=true | all-gather | bytes 69632 | tf_op jit(solution)/shard_map/all_gather | solution.py:151
  150.5 36.6 %all_gather.23 = f32[2048,8]{0,1:T(8,128)S(1)} all-gather(f32[128,8]{0,1:T(8,128)S(1)} %bitcast.287), channel_id=1, replica_groups=mesh['ctx'=16,'dp'=2] {'ctx'}, dimensions={0}, use_global_device_ids=true | all-gather | bytes 69632 | tf_op jit(solution)/shard_map/all_gather | solution.py:152
  187.1 14.0 %while.54 = (s32[]{:T(128)}, f32[128,8,128]{0,2,1:T(8,128)}, bf16[4,512,128]{2,1,0:T(8,128)(2,1)S(1)}, s32[4,512]{1,0:T(4,128)S(1)}, s32[4,512]{1,0:T(4,128)S(1)...) while((s32[]{:T(128)}, f32[128,8,128]{0,2,1:T(8,128)}, ...), condition=%wide.region_11.12_spmd.clone, body=%wide.region_10.11_spmd.clone.sunk | while | flops 406258304 | bytes 6315182 | solution.py:140
  187.8 2.7 %fusion.138 = f32[128,8,128]{0,2,1:T(8,128)} fusion(f32[512,128,8]{1,0,2:T(8,128)S(1)} %fusion.136, bf16[128,8,128]{2,0,1:T(8,128)(2,1)} %get-tuple-element.1265, f32[8,128]{1,0:T(8,128)S(1)} %get-tuple-element.1266, f32[8,128]{1,0:T(8,128)S(1)} %get-tuple-element.1263, pred[128,512]{0,1:T(8,128)(4,1)S(1)} %compare_and_fusion.10, ...), kind=kOutput, calls=%fused_computation.52.clone.1 | convolution fusion | flops 271843328 | bytes 3745280 | tf_op jit(solution)/shard_map/while/body/eval_jaxpr/htk,kd->thd/dot_general | solution.py:136
  191.1 2.9 %fusion.138 = f32[128,8,128]{0,2,1:T(8,128)} fusion(f32[512,128,8]{1,0,2:T(8,128)S(1)} %fusion.136, bf16[128,8,128]{2,0,1:T(8,128)(2,1)} %get-tuple-element.1265, f32[8,128]{1,0:T(8,128)S(1)} %get-tuple-element.1266, f32[8,128]{1,0:T(8,128)S(1)} %get-tuple-element.1263, pred[128,512]{0,1:T(8,128)(4,1)S(1)} %compare_and_fusion.10, ...), kind=kOutput, calls=%fused_computation.52.clone.1 | convolution fusion | flops 271843328 | bytes 3745280 | tf_op jit(solution)/shard_map/while/body/eval_jaxpr/htk,kd->thd/dot_general | solution.py:136
  194.7 2.9 %fusion.138 = f32[128,8,128]{0,2,1:T(8,128)} fusion(f32[512,128,8]{1,0,2:T(8,128)S(1)} %fusion.136, bf16[128,8,128]{2,0,1:T(8,128)(2,1)} %get-tuple-element.1265, f32[8,128]{1,0:T(8,128)S(1)} %get-tuple-element.1266, f32[8,128]{1,0:T(8,128)S(1)} %get-tuple-element.1263, pred[128,512]{0,1:T(8,128)(4,1)S(1)} %compare_and_fusion.10, ...), kind=kOutput, calls=%fused_computation.52.clone.1 | convolution fusion | flops 271843328 | bytes 3745280 | tf_op jit(solution)/shard_map/while/body/eval_jaxpr/htk,kd->thd/dot_general | solution.py:136
  198.2 2.9 %fusion.138 = f32[128,8,128]{0,2,1:T(8,128)} fusion(f32[512,128,8]{1,0,2:T(8,128)S(1)} %fusion.136, bf16[128,8,128]{2,0,1:T(8,128)(2,1)} %get-tuple-element.1265, f32[8,128]{1,0:T(8,128)S(1)} %get-tuple-element.1266, f32[8,128]{1,0:T(8,128)S(1)} %get-tuple-element.1263, pred[128,512]{0,1:T(8,128)(4,1)S(1)} %compare_and_fusion.10, ...), kind=kOutput, calls=%fused_computation.52.clone.1 | convolution fusion | flops 271843328 | bytes 3745280 | tf_op jit(solution)/shard_map/while/body/eval_jaxpr/htk,kd->thd/dot_general | solution.py:136
  201.1 42.7 %while.55 = (s32[]{:T(128)}, f32[128,128]{1,0:T(8,128)S(1)}, f32[128,128]{1,0:T(8,128)S(1)}, s32[4,512]{1,0:T(4,128)S(1)}, s32[128]{0:T(128)S(1)}, /*index=5*/s3...) while((s32[]{:T(128)}, f32[128,128]{1,0:T(8,128)S(1)}, ...), condition=%wide.region_13.14_spmd.clone, body=%wide.region_12.13_spmd.clone.sunk | while | flops 540803712 | bytes 19449588 | solution.py:196
  202.5 1.7 constant_dynamic-slice_fusion.18
  206.1 2.1 fusion.147
  208.2 2.9 %fusion.148 = f32[128,128]{1,0:T(8,128)S(1)} fusion(bf16[512,8,128]{0,2,1:T(8,128)(2,1)} %bitcast.268, f32[8,512,128]{2,1,0:T(8,128)S(1)} %fusion.147, bf16[512,8,128]{0,2,1:T(8,128)(2,1)S(1)} %bitcast.265, f32[8,512]{1,0:T(8,128)S(1)} %get-tuple-element.1150, f32[128,128]{1,0:T(8,128)S(1)} %get-tuple-element.1288, ...), kind=kOutput, calls=%fused_computation.84.clone.1 | convolution fusion | flops 270041088 | bytes 4374529 | tf_op jit(solution)/shard_map/while/body/eval_jaxpr/hrk,rhd->kd/dot_general | solution.py:191
  216.8 2.1 fusion.147
  218.9 2.9 %fusion.148 = f32[128,128]{1,0:T(8,128)S(1)} fusion(bf16[512,8,128]{0,2,1:T(8,128)(2,1)} %bitcast.268, f32[8,512,128]{2,1,0:T(8,128)S(1)} %fusion.147, bf16[512,8,128]{0,2,1:T(8,128)(2,1)S(1)} %bitcast.265, f32[8,512]{1,0:T(8,128)S(1)} %get-tuple-element.1150, f32[128,128]{1,0:T(8,128)S(1)} %get-tuple-element.1288, ...), kind=kOutput, calls=%fused_computation.84.clone.1 | convolution fusion | flops 270041088 | bytes 4374529 | tf_op jit(solution)/shard_map/while/body/eval_jaxpr/hrk,rhd->kd/dot_general | solution.py:191
  223.9 1.7 constant_dynamic-slice_fusion.18
  227.5 2.1 fusion.147
  229.6 2.9 %fusion.148 = f32[128,128]{1,0:T(8,128)S(1)} fusion(bf16[512,8,128]{0,2,1:T(8,128)(2,1)} %bitcast.268, f32[8,512,128]{2,1,0:T(8,128)S(1)} %fusion.147, bf16[512,8,128]{0,2,1:T(8,128)(2,1)S(1)} %bitcast.265, f32[8,512]{1,0:T(8,128)S(1)} %get-tuple-element.1150, f32[128,128]{1,0:T(8,128)S(1)} %get-tuple-element.1288, ...), kind=kOutput, calls=%fused_computation.84.clone.1 | convolution fusion | flops 270041088 | bytes 4374529 | tf_op jit(solution)/shard_map/while/body/eval_jaxpr/hrk,rhd->kd/dot_general | solution.py:191
  238.2 2.1 fusion.147
  240.2 2.9 %fusion.148 = f32[128,128]{1,0:T(8,128)S(1)} fusion(bf16[512,8,128]{0,2,1:T(8,128)(2,1)} %bitcast.268, f32[8,512,128]{2,1,0:T(8,128)S(1)} %fusion.147, bf16[512,8,128]{0,2,1:T(8,128)(2,1)S(1)} %bitcast.265, f32[8,512]{1,0:T(8,128)S(1)} %get-tuple-element.1150, f32[128,128]{1,0:T(8,128)S(1)} %get-tuple-element.1288, ...), kind=kOutput, calls=%fused_computation.84.clone.1 | convolution fusion | flops 270041088 | bytes 4374529 | tf_op jit(solution)/shard_map/while/body/eval_jaxpr/hrk,rhd->kd/dot_general | solution.py:191
  247.1 2.4 reduce-scatter.5.cloned.1.call-done
  249.5 11.2 %reduce-scatter.3.cloned.1.call-done = bf16[64,128]{1,0:T(8,128)(2,1)} async-done(((bf16[128,128]{1,0:T(8,128)(2,1)}), bf16[64,128]{1,0:T(8,128)(2,1)}) %reduce-scatter.3.cloned.1.call-update) | async-done | bytes 16400 | tf_op jit(solution)/shard_map/reduce_scatter | solution.py:198
  (157 shorter events, 40.7 us)
Async XLA Ops:
  7.2 194.0 %all-gather.3.cloned.1.call-start = ((), (), s32[]{:S(2)}) async-start(), calls=%async_computation.2 | async-start | bytes 4456448 | tf_op jit(solution)/shard_map/all_gather | solution.py:147
  7.9 193.2 %all-gather.5.cloned.1.call-start = ((), (), s32[]{:S(2)}) async-start(), calls=%async_computation.3 | async-start | bytes 4456448 | tf_op jit(solution)/shard_map/all_gather | solution.py:148
  8.6 240.9 %reduce-scatter.5.cloned.1.call-start = ((), (), s32[]{:S(2)}) async-start(), calls=%async_computation.5 | async-start | bytes 49152 | tf_op jit(solution)/shard_map/reduce_scatter | solution.py:201
  58.3 4.9 %copy-start.1 = (bf16[128,1024]{1,0:T(8,128)(2,1)S(1)}, bf16[128,1024]{1,0:T(8,128)(2,1)}, u32[]{:S(2)}) copy-start(bf16[128,1024]{1,0:T(8,128)(2,1)} %param.16) | copy-start | bytes 786436
  58.3 5.9 %copy-start = (bf16[128,128]{1,0:T(8,128)(2,1)S(1)}, bf16[128,128]{1,0:T(8,128)(2,1)}, u32[]{:S(2)}) copy-start(bf16[128,128]{1,0:T(8,128)(2,1)} %param.15) | copy-start | bytes 98308
  111.4 0.8 copy-start.2
  201.1 0.5 copy-start.3
  211.1 0.7 copy-start.4
  211.8 0.5 copy-start.3
  221.8 0.7 copy-start.4
  222.5 0.5 copy-start.3
  232.5 0.7 copy-start.4
  233.2 0.5 copy-start.3
  243.2 0.7 copy-start.4
  244.5 16.3 %reduce-scatter.3.cloned.1.call-start = ((), (), s32[]{:S(2)}) async-start(), calls=%async_computation.4 | async-start | bytes 49152 | tf_op jit(solution)/shard_map/reduce_scatter | solution.py:198
Sparse Core Ops, SparseCore 0:
  10.8 85.3 all-gather.2
  98.9 77.1 all-gather.4
  244.6 4.9 reduce-scatter.4
  252.2 8.5 reduce-scatter.2
where the time goes:
time: 268 us; the launch traced here: 267 us
  blocking collectives  164 us (61%)
  matrix products  41 us (15%)
  local copies, waits for them, and re-layouts  21.6 us (8%)
  waiting for transfers between devices  15.1 us (6%)
  between operations  14 us (5%)
  other arithmetic  11.3 us (4%)
    all_gather x1, blocking collectives, body(): lax.all_gather(keys, 'ctx', axis=0, tiled=True)  47 us
    all_gather x1, blocking collectives, body(): lax.all_gather(values, 'ctx', axis=0, tiled=True)  41.9 us
    all_gather x1, blocking collectives, body(): lax.all_gather(lse_rows, 'ctx', axis=0, tiled=True)  38.1 us
    all_gather x1, blocking collectives, body(): lax.all_gather(delta_rows, 'ctx', axis=0, tiled=True)  36.6 us
    dynamic_slice x12, local copies, waits for them, and re-layouts, body(): lax.scan(key_step, (zero_grads, zero_grads), query_stack)  14.5 us
    dot_general x4, matrix products, key_step(): jnp.einsum('hrk,rhd->kd', dlogits, query_split, preferred_element_type=jn...  11.7 us
    dot_general x4, matrix products, query_step(): jnp.einsum('htk,kd->thd', dlogits, key_block, preferred_element_type=jnp....  11.4 us
    reduce_scatter x1, waiting for transfers between devices, body(): lax.psum_scatter((score_scale * key_part).astype(jnp.bfloat16), 'dp', sca...  11.2 us
  transfers between devices with their start and end apart: 4, of which 2 were waited for; matrix products, arithmetic and copies ran while one was open for 11% of the time, Pallas kernels for 0%

commit v1 on v0

v1 whole, which is shorter than its diff:
```python
import functools
import math

import jax
import jax.numpy as jnp
from jax import lax
from jax.experimental import pallas as pl
from jax.experimental.pallas import tpu as pltpu
from jax.sharding import PartitionSpec as P

masked_value = -1e30


def span_row(span, ctx_count, span_rows):
    low = span < ctx_count
    return (span if low else 2 * ctx_count - 1 - span) * 2 * span_rows + (0 if low else span_rows)


def attend_kernel(
    ctx_count,
    tile,
    lengths_ref,
    q_ref,
    g_ref,
    kv_ref,
    dq_ref,
    dkv_ref,
    ordered_ref,
    kt_ref,
    acc_ref,
    stack_ref,
    flip_ref,
    s_ref,
    dp_ref,
    dqt_ref,
):
    tok_rows, width = q_ref.shape
    head_width = kv_ref.shape[1] // 2
    head_count = width // head_width
    span_rows = tok_rows // 2
    span_count = 2 * ctx_count
    seq = span_count * span_rows
    cols = head_count * span_rows
    scale = head_width ** (-0.5)
    ctx_index = lax.axis_index("ctx")

    for span in range(span_count):
        ordered_ref[pl.ds(span * span_rows, span_rows), :] = kv_ref[
            pl.ds(span_row(span, ctx_count, span_rows), span_rows), :
        ]
    for part in range(seq // tile):
        rows = pl.ds(part * tile, tile)
        kt_ref[:, rows] = ordered_ref[rows, :head_width].T
    acc_ref[...] = jnp.zeros_like(acc_ref)

    for half in range(2):
        rows = pl.ds(half * span_rows, span_rows)
        for head in range(head_count):
            lanes = pl.ds(head * head_width, head_width)
            out_rows = pl.ds(head * span_rows, span_rows)
            stack_ref[0, out_rows, :] = q_ref[rows, lanes]
            stack_ref[1, out_rows, :] = g_ref[rows, lanes]
        flip_ref[0] = stack_ref[0].T
        flip_ref[1] = stack_ref[1].T
        span = ctx_index if half == 0 else span_count - 1 - ctx_index
        first = span * span_rows
        query_pos = first + lax.rem(
            lax.broadcasted_iota(jnp.int32, (1, cols), 1), jnp.int32(span_rows)
        )
        doc_start = jnp.zeros((1, cols), jnp.int32)
        first_key = jnp.int32(0)
        end = jnp.int32(0)
        for doc in range(lengths_ref.shape[0]):
            end = end + lengths_ref[doc]
            doc_start = jnp.where(query_pos >= end, end, doc_start)
            first_key = jnp.where(first >= end, end, first_key)
        tile_low = first_key // tile
        tile_high = (first + span_rows + tile - 1) // tile

        def logits_step(index, top):
            rows = pl.ds(pl.multiple_of(index * tile, tile), tile)
            logits = jnp.dot(
                ordered_ref[rows, :head_width], flip_ref[0], preferred_element_type=jnp.float32
            )
            key_pos = index * tile + lax.broadcasted_iota(jnp.int32, (tile, cols), 0)
            live = (key_pos >= doc_start) & (key_pos <= query_pos)
            logits = jnp.where(live, logits * scale, masked_value)
            s_ref[rows, :] = logits
            return jnp.maximum(top, jnp.max(logits, axis=0, keepdims=True))

        top = lax.fori_loop(
            tile_low, tile_high, logits_step, jnp.full((1, cols), masked_value, jnp.float32)
        )

        def sums_step(index, state):
            total, mixed = state
            rows = pl.ds(pl.multiple_of(index * tile, tile), tile)
            terms = jnp.exp(s_ref[rows, :] - top)
            dweights = jnp.dot(
                ordered_ref[rows, head_width:], flip_ref[1], preferred_element_type=jnp.float32
            )
            s_ref[rows, :] = terms
            dp_ref[rows, :] = dweights
            return (
                total + jnp.sum(terms, axis=0, keepdims=True),
                mixed + jnp.sum(terms * dweights, axis=0, keepdims=True),
            )

        zero = jnp.zeros((1, cols), jnp.float32)
        total, mixed = lax.fori_loop(tile_low, tile_high, sums_step, (zero, zero))
        inverse = 1.0 / total
        delta = mixed * inverse
        dqt_ref[...] = jnp.zeros_like(dqt_ref)

        def grads_step(index, carry):
            rows = pl.ds(pl.multiple_of(index * tile, tile), tile)
            weights = s_ref[rows, :] * inverse
            dlogits = (weights * (dp_ref[rows, :] - delta)).astype(jnp.bfloat16)
            acc_ref[rows, head_width:] += jnp.dot(
                weights.astype(jnp.bfloat16), stack_ref[1], preferred_element_type=jnp.float32
            )
            acc_ref[rows, :head_width] += jnp.dot(
                dlogits, stack_ref[0], preferred_element_type=jnp.float32
            )
            dqt_ref[...] += jnp.dot(kt_ref[:, rows], dlogits, preferred_element_type=jnp.float32)
            return carry

        lax.fori_loop(tile_low, tile_high, grads_step, 0)
        dq = (scale * dqt_ref[...]).T.astype(jnp.bfloat16)
        for head in range(head_count):
            dq_ref[rows, pl.ds(head * head_width, head_width)] = dq[
                head * span_rows : (head + 1) * span_rows
            ]

    for span in range(span_count):
        rows = pl.ds(span * span_rows, span_rows)
        out_rows = pl.ds(span_row(span, ctx_count, span_rows), span_rows)
        dkv_ref[out_rows, :head_width] = (scale * acc_ref[rows, :head_width]).astype(jnp.bfloat16)
        dkv_ref[out_rows, head_width:] = acc_ref[rows, head_width:].astype(jnp.bfloat16)


def attend(ctx_count, doc_lengths, queries, out_grads, kv_all):
    tok_rows, width = queries.shape
    seq, kv_width = kv_all.shape
    head_width = kv_width // 2
    span_rows = tok_rows // 2
    cols = width // head_width * span_rows
    tile = min(256, seq)
    vmem = pl.BlockSpec(memory_space=pltpu.VMEM)
    return pl.pallas_call(
        functools.partial(attend_kernel, ctx_count, tile),
        out_shape=(
            jax.ShapeDtypeStruct((tok_rows, width), jnp.bfloat16),
            jax.ShapeDtypeStruct((seq, kv_width), jnp.bfloat16),
        ),
        in_specs=[pl.BlockSpec(memory_space=pltpu.SMEM), vmem, vmem, vmem],
        out_specs=(vmem, vmem),
        scratch_shapes=[
            pltpu.VMEM((seq, kv_width), jnp.bfloat16),
            pltpu.VMEM((head_width, seq), jnp.bfloat16),
            pltpu.VMEM((seq, kv_width), jnp.float32),
            pltpu.VMEM((2, cols, head_width), jnp.bfloat16),
            pltpu.VMEM((2, head_width, cols), jnp.bfloat16),
            pltpu.VMEM((seq, cols), jnp.float32),
            pltpu.VMEM((seq, cols), jnp.float32),
            pltpu.VMEM((head_width, cols), jnp.float32),
        ],
        compiler_params=pltpu.CompilerParams(vmem_limit_bytes=40 * 1024 * 1024),
    )(doc_lengths, queries, out_grads, kv_all)


def body(queries, keys, values, out_grads, doc_lengths):
    ctx_count = lax.axis_size("ctx")
    dp_count = lax.axis_size("dp")
    tok_rows, head_width = keys.shape
    kv_all = lax.all_gather(
        jnp.concatenate([keys, values], axis=1), "ctx", axis=0, tiled=True
    )
    query_grads, kv_parts = attend(ctx_count, doc_lengths, queries, out_grads, kv_all)
    received = lax.all_to_all(kv_parts, ("ctx", "dp"), split_axis=0, concat_axis=0, tiled=True)
    shares = received.reshape(ctx_count * dp_count, tok_rows // dp_count, 2 * head_width)
    kv_grads = jnp.sum(shares.astype(jnp.float32), axis=0).astype(jnp.bfloat16)
    return (query_grads, kv_grads[:, :head_width], kv_grads[:, head_width:])


def solution(mesh):
    return jax.shard_map(
        body,
        mesh=mesh,
        in_specs=(P("ctx", "dp"), P("ctx", None), P("ctx", None), P("ctx", "dp"), P()),
        out_specs=(P("ctx", "dp"), P(("ctx", "dp"), None), P(("ctx", "dp"), None)),
        check_vma=False,
    )
```

time: 268 us -> 117 us (0.44)
  blocking collectives: 164 us -> 35.1 us
  waiting for transfers between devices: 15.1 us -> 60.7 us
  matrix products: 41 us -> 0 us
  local copies, waits for them, and re-layouts: 21.6 us -> 3.74 us
  other arithmetic: 11.3 us -> 1.57 us
  Pallas kernels: 0 us -> 3.57 us
    all_gather x4 -> x0, blocking collectives: 164 us -> none  [the longest x1 47 us: body(): lax.all_gather(keys, 'ctx', axis=0, tiled=True)]
    all_gather x2 -> x1, waiting for transfers between devices: 0.01 us -> 60.7 us  [body(): lax.all_gather(jnp.concatenate([keys, values], axis=1), 'ctx', axis=0, ti...]
    dot_general x28 -> x0, matrix products: 41 us -> none  [the longest x4 11.7 us: key_step(): jnp.einsum('hrk,rhd->kd', dlogits, query_split, preferred_element_type=jn...]
    all_to_all x0 -> x1, blocking collectives: none -> 35.1 us  [body(): lax.all_to_all(kv_parts, ('ctx', 'dp'), split_axis=0, concat_axis=0, tile...]
    dynamic_slice x28 -> x0, local copies, waits for them, and re-layouts: 14.6 us -> none  [the longest x12 14.5 us: body(): lax.scan(key_step, (zero_grads, zero_grads), query_stack)]
    reduce_scatter x2 -> x0, waiting for transfers between devices: 13.7 us -> none  [the longest x1 11.2 us: body(): lax.psum_scatter((score_scale * key_part).astype(jnp.bfloat16), 'dp', sca...]
    and x16 -> x0, other arithmetic: 5.86 us -> none  [the longest x4 3.42 us: key_step(): query_alive[:, None] & (own_pos[None, :] <= query_pos[:, None])]
    pallas_call x0 -> x1, Pallas kernels: none -> 3.57 us  [attend(): pl.pallas_call(functools.partial(attend_kernel, ctx_count, tile), out_sha...]
  transfers between devices with their start and end apart: 4 -> 1, of which waited for: 2 -> 1; matrix products, arithmetic and copies ran while one was open for 11% -> 0% of each run, Pallas kernels for 0% -> 0%
where the time goes in v1:
time: 117 us; the launch traced here: 119 us
  waiting for transfers between devices  60.7 us (52%)
  blocking collectives  35.1 us (30%)
  between operations  14 us (12%)
  local copies, waits for them, and re-layouts  3.74 us (3%)
  Pallas kernels  3.57 us (3%)
  other arithmetic  1.57 us (1%)
    all_gather x1, waiting for transfers between devices, body(): lax.all_gather(jnp.concatenate([keys, values], axis=1), 'ctx', axis=0, ti...  60.7 us
    all_to_all x1, blocking collectives, body(): lax.all_to_all(kv_parts, ('ctx', 'dp'), split_axis=0, concat_axis=0, tile...  35.1 us
    pallas_call x1, Pallas kernels, attend(): pl.pallas_call(functools.partial(attend_kernel, ctx_count, tile), out_sha...  3.57 us
    unnamed x8, local copies, waits for them, and re-layouts  3.13 us
  transfers between devices with their start and end apart: 1, of which 1 were waited for; matrix products, arithmetic and copies ran while one was open for 0% of the time, Pallas kernels for 0%

profile of v1, /device:TPU:0, one launch (start us, length us, event | category | flops | bytes accessed | tf_op | source)
XLA Modules:
  0.0 118.7 jit_solution(6196233175663256297)
XLA Ops:
  7.2 0.0 all-gather.2.cloned.1.call-start
  7.2 1.4 %pad_maximum_fusion = bf16[128,256]{1,0:T(8,128)(2,1)} fusion(bf16[128,128]{1,0:T(8,128)(2,1)} %param.7, bf16[128,128]{1,0:T(8,128)(2,1)} %param.6), kind=kLoop, calls=%fused_computation | loop fusion | flops 131072 | bytes 131072 | tf_op jit(solution)/shard_map/concatenate | solution.py:177
  8.6 0.0 copy-start.3
  8.6 0.0 all-gather.2.cloned.1.call-update
  8.7 60.7 %all-gather.2.cloned.1.call-done.kv_ref = bf16[2048,256]{1,0:T(8,128)(2,1)} async-done(((bf16[128,256]{1,0:T(8,128)(2,1)}), bf16[2048,256]{1,0:T(8,128)(2,1)}) %all-gather.2.cloned.1.call-update) | async-done | bytes 1048592 | tf_op jit(solution)/shard_map/all_gather | solution.py:176
  69.3 0.0 copy-done.3
  69.3 0.0 copy-start
  69.3 1.2 %copy-done = bf16[2048,256]{1,0:T(8,128)(2,1)S(1)} copy-done((bf16[2048,256]{1,0:T(8,128)(2,1)S(1)}, bf16[2048,256]{1,0:T(8,128)(2,1)}, u32[]{:S(2)}) %copy-start) | copy-done | bytes 1048600
  70.6 0.0 copy-start.1
  70.6 0.9 copy-done.1
  71.5 0.0 copy-start.2
  71.5 0.9 copy-done.2
  72.5 3.6 %shard_map.76 = (bf16[128,1024]{1,0:T(8,128)(2,1)}, bf16[2048,256]{1,0:T(8,128)(2,1)S(1)}) custom-call(s32[8]{0:T(128)S(1)} %copy-done.3, bf16[128,1024]{1,0:T(8,128)(2,1)S(1)} %copy-done.1, bf16[128,1024]{1,0:T(8,128)(2,1)S(1)} %copy-done.2, bf16[2048,256]{1,0:T(8,128)(2,1)S(1)} %copy-done), custom_call_target="tpu_custom_call" | custom-call | tf_op jit(solution)/shard_map/pallas_call | solution.py:150
  76.0 35.1 %all_to_all.9 = bf16[32,64,256]{2,1,0:T(8,128)(2,1)S(1)} all-to-all(bf16[32,64,256]{2,1,0:T(8,128)(2,1)S(1)} %bitcast.1), channel_id=1, replica_groups=mesh['ctx'=16,'dp'=2] {'ctx','dp'}, dimensions={0} | all-to-all | bytes 2097152 | tf_op jit(solution)/shard_map/all_to_all | solution.py:180
  111.1 0.2 reduce_sum.12
  111.3 0.6 fusion
Async XLA Ops:
  7.2 62.2 %all-gather.2.cloned.1.call-start = ((), (), s32[]{:S(2)}) async-start(), calls=%async_computation.1 | async-start | bytes 1114112 | tf_op jit(solution)/shard_map/all_gather | solution.py:176
  8.6 60.7 %copy-start.3 = (s32[8]{0:T(128)S(1)}, s32[8]{0:T(128)}, u32[]{:S(2)}) copy-start(s32[8]{0:T(128)} %lengths_ref.1) | copy-start | bytes 100
  69.3 1.2 %copy-start = (bf16[2048,256]{1,0:T(8,128)(2,1)S(1)}, bf16[2048,256]{1,0:T(8,128)(2,1)}, u32[]{:S(2)}) copy-start(bf16[2048,256]{1,0:T(8,128)(2,1)} %all-gather.2.cloned.1.call-done.kv_ref) | copy-start | bytes 3145732
  70.6 0.9 copy-start.1
  71.5 0.9 copy-start.2
Sparse Core Ops, SparseCore 0:
  11.3 57.9 all-gather.1

commit v2 on v1

--- a/solution.py
+++ b/solution.py
@@ -11,31 +11,34 @@
 masked_value = -1e30
 
 
-def span_row(span, ctx_count, span_rows):
-    low = span < ctx_count
-    return (span if low else 2 * ctx_count - 1 - span) * 2 * span_rows + (0 if low else span_rows)
+def part_position(ctx_index, dp_index, ctx_count, part_rows, span_rows):
+    start = dp_index * part_rows
+    low = ctx_index * span_rows + start
+    high = (2 * ctx_count - 1 - ctx_index) * span_rows + start - span_rows
+    return pl.multiple_of(jnp.where(start < span_rows, low, high), part_rows)
 
 
 def attend_kernel(
     ctx_count,
+    dp_count,
+    inner,
     tile,
     lengths_ref,
     q_ref,
     g_ref,
-    kv_ref,
-    dq_ref,
-    dkv_ref,
-    ordered_ref,
-    kt_ref,
-    acc_ref,
-    stack_ref,
-    flip_ref,
-    s_ref,
-    dp_ref,
-    dqt_ref,
+    *refs,
 ):
+    outer = ctx_count // inner
+    piece_count = dp_count * inner
+    kv_refs = refs[:piece_count]
+    dq_ref = refs[piece_count]
+    dkv_refs = refs[piece_count + 1 : 2 * piece_count + 1]
+    ordered_ref, kt_ref, acc_ref, stack_ref, flip_ref, s_ref, dp_ref, dqt_ref = refs[
+        2 * piece_count + 1 :
+    ]
     tok_rows, width = q_ref.shape
-    head_width = kv_ref.shape[1] // 2
+    part_rows = tok_rows // dp_count
+    head_width = kv_refs[0].shape[1] // 2
     head_count = width // head_width
     span_rows = tok_rows // 2
     span_count = 2 * ctx_count
@@ -44,10 +47,19 @@
     scale = head_width ** (-0.5)
     ctx_index = lax.axis_index("ctx")
 
-    for span in range(span_count):
-        ordered_ref[pl.ds(span * span_rows, span_rows), :] = kv_ref[
-            pl.ds(span_row(span, ctx_count, span_rows), span_rows), :
-        ]
+    dp_index = lax.axis_index("dp")
+
+    def blocks():
+        for piece in range(piece_count):
+            for block in range(outer):
+                owner = ctx_index ^ (piece % inner) ^ (block * inner)
+                position = part_position(
+                    owner, dp_index ^ (piece // inner), ctx_count, part_rows, span_rows
+                )
+                yield piece, pl.ds(block * part_rows, part_rows), pl.ds(position, part_rows)
+
+    for piece, here, ordered in blocks():
+        ordered_ref[ordered, :] = kv_refs[piece][here, :]
     for part in range(seq // tile):
         rows = pl.ds(part * tile, tile)
         kt_ref[:, rows] = ordered_ref[rows, :head_width].T
@@ -132,29 +144,28 @@
                 head * span_rows : (head + 1) * span_rows
             ]
 
-    for span in range(span_count):
-        rows = pl.ds(span * span_rows, span_rows)
-        out_rows = pl.ds(span_row(span, ctx_count, span_rows), span_rows)
-        dkv_ref[out_rows, :head_width] = (scale * acc_ref[rows, :head_width]).astype(jnp.bfloat16)
-        dkv_ref[out_rows, head_width:] = acc_ref[rows, head_width:].astype(jnp.bfloat16)
-
-
-def attend(ctx_count, doc_lengths, queries, out_grads, kv_all):
+    for piece, here, ordered in blocks():
+        dkv_refs[piece][here, :head_width] = (scale * acc_ref[ordered, :head_width]).astype(
+            jnp.bfloat16
+        )
+        dkv_refs[piece][here, head_width:] = acc_ref[ordered, head_width:].astype(jnp.bfloat16)
+
+
+def attend(ctx_count, dp_count, inner, doc_lengths, queries, out_grads, pieces):
     tok_rows, width = queries.shape
-    seq, kv_width = kv_all.shape
+    kv_width = pieces[0].shape[1]
     head_width = kv_width // 2
     span_rows = tok_rows // 2
+    seq = ctx_count * tok_rows
     cols = width // head_width * span_rows
     tile = min(256, seq)
     vmem = pl.BlockSpec(memory_space=pltpu.VMEM)
-    return pl.pallas_call(
-        functools.partial(attend_kernel, ctx_count, tile),
-        out_shape=(
-            jax.ShapeDtypeStruct((tok_rows, width), jnp.bfloat16),
-            jax.ShapeDtypeStruct((seq, kv_width), jnp.bfloat16),
-        ),
-        in_specs=[pl.BlockSpec(memory_space=pltpu.SMEM), vmem, vmem, vmem],
-        out_specs=(vmem, vmem),
+    results = pl.pallas_call(
+        functools.partial(attend_kernel, ctx_count, dp_count, inner, tile),
+        out_shape=[jax.ShapeDtypeStruct((tok_rows, width), jnp.bfloat16)]
+        + [jax.ShapeDtypeStruct(piece.shape, jnp.bfloat16) for piece in pieces],
+        in_specs=[pl.BlockSpec(memory_space=pltpu.SMEM)] + [vmem] * (2 + len(pieces)),
+        out_specs=[vmem] * (1 + len(pieces)),
         scratch_shapes=[
             pltpu.VMEM((seq, kv_width), jnp.bfloat16),
             pltpu.VMEM((head_width, seq), jnp.bfloat16),
@@ -166,20 +177,53 @@
             pltpu.VMEM((head_width, cols), jnp.float32),
         ],
         compiler_params=pltpu.CompilerParams(vmem_limit_bytes=40 * 1024 * 1024),
-    )(doc_lengths, queries, out_grads, kv_all)
+    )(doc_lengths, queries, out_grads, *pieces)
+    return results[0], results[1:]
+
+
+def swap(value, axis, offset):
+    pairs = [(index, index ^ offset) for index in range(lax.axis_size(axis))]
+    return lax.ppermute(value, axis, pairs)
+
+
+def total_of(terms):
+    return sum(term.astype(jnp.float32) for term in terms)
 
 
 def body(queries, keys, values, out_grads, doc_lengths):
     ctx_count = lax.axis_size("ctx")
     dp_count = lax.axis_size("dp")
+    inner = math.gcd(4, ctx_count)
+    outer = ctx_count // inner
     tok_rows, head_width = keys.shape
-    kv_all = lax.all_gather(
-        jnp.concatenate([keys, values], axis=1), "ctx", axis=0, tiled=True
-    )
-    query_grads, kv_parts = attend(ctx_count, doc_lengths, queries, out_grads, kv_all)
-    received = lax.all_to_all(kv_parts, ("ctx", "dp"), split_axis=0, concat_axis=0, tiled=True)
-    shares = received.reshape(ctx_count * dp_count, tok_rows // dp_count, 2 * head_width)
-    kv_grads = jnp.sum(shares.astype(jnp.float32), axis=0).astype(jnp.bfloat16)
+    part_rows = tok_rows // dp_count
+    own = lax.dynamic_slice_in_dim(
+        jnp.concatenate([keys, values], axis=1), lax.axis_index("dp") * part_rows, part_rows, 0
+    )
+    line = jnp.concatenate(
+        [own] + [swap(own, "ctx", block * inner) for block in range(1, outer)], axis=0
+    )
+    plane = [line] + [swap(line, "ctx", offset) for offset in range(1, inner)]
+    pieces = plane + [
+        swap(piece, "dp", offset) for offset in range(1, dp_count) for piece in plane
+    ]
+    query_grads, parts = attend(
+        ctx_count, dp_count, inner, doc_lengths, queries, out_grads, pieces
+    )
+    plane_sums = [
+        total_of(
+            [parts[offset]]
+            + [swap(parts[far * inner + offset], "dp", far) for far in range(1, dp_count)]
+        ).astype(jnp.bfloat16)
+        for offset in range(inner)
+    ]
+    line_sum = total_of(
+        [plane_sums[0]] + [swap(plane_sums[offset], "ctx", offset) for offset in range(1, inner)]
+    ).astype(jnp.bfloat16)
+    blocks = [line_sum[block * part_rows : (block + 1) * part_rows] for block in range(outer)]
+    kv_grads = total_of(
+        [blocks[0]] + [swap(blocks[block], "ctx", block * inner) for block in range(1, outer)]
+    ).astype(jnp.bfloat16)
     return (query_grads, kv_grads[:, :head_width], kv_grads[:, head_width:])
 
 

time: 117 us -> 48.6 us (0.42); the launches traced: 119 us -> 48.1 us
  waiting for transfers between devices: 60.7 us -> 19.7 us
  blocking collectives: 35.1 us -> 0 us
  starting transfers between devices: 0.04 us -> 18.1 us
  between operations: 14 us -> 0.7 us
  Pallas kernels: 3.57 us -> 7 us
  local copies, waits for them, and re-layouts: 3.74 us -> 1.58 us
    all_gather x1 -> x0, waiting for transfers between devices: 60.7 us -> none  [body(): lax.all_gather(jnp.concatenate([keys, values], axis=1), 'ctx', axis=0, ti...]
    all_to_all x1 -> x0, blocking collectives: 35.1 us -> none  [body(): lax.all_to_all(kv_parts, ('ctx', 'dp'), split_axis=0, concat_axis=0, tile...]
    ppermute x0 -> x20, waiting for transfers between devices: none -> 19.7 us  [swap(): return lax.ppermute(value, axis, pairs)]
    ppermute x0 -> x20, starting transfers between devices: none -> 18.1 us  [swap(): return lax.ppermute(value, axis, pairs)]
    pallas_call x1, Pallas kernels: 3.57 us -> 7 us  [attend(): pl.pallas_call(functools.partial(attend_kernel, ctx_count, dp_count, inne...]
    unnamed x8 -> x6, local copies, waits for them, and re-layouts: 3.13 us -> 0.96 us
  transfers between devices with their start and end apart: 1 -> 20, of which waited for: 1 -> 13; matrix products, arithmetic and copies ran while one was open for 0% -> 0% of each run, Pallas kernels for 0% -> 0%
where the time goes in v2:
time: 48.6 us; the launch traced here: 48.1 us
  waiting for transfers between devices  19.7 us (41%)
  starting transfers between devices  18.1 us (37%)
  Pallas kernels  7 us (14%)
  local copies, waits for them, and re-layouts  1.58 us (3%)
  other arithmetic  1 us (2%)
  between operations  0.7 us (1%)
    ppermute x20, waiting for transfers between devices, swap(): return lax.ppermute(value, axis, pairs)  19.7 us
    ppermute x20, starting transfers between devices, swap(): return lax.ppermute(value, axis, pairs)  18.1 us
    pallas_call x1, Pallas kernels, attend(): pl.pallas_call(functools.partial(attend_kernel, ctx_count, dp_count, inne...  7 us
  transfers between devices with their start and end apart: 20, of which 13 were waited for; matrix products, arithmetic and copies ran while one was open for 0% of the time, Pallas kernels for 0%

profile of v2, /device:TPU:0, one launch (start us, length us, event | category | flops | bytes accessed | tf_op | source)
XLA Modules:
  0.0 48.1 jit_solution(10249632597425220577)
XLA Ops:
  0.6 0.8 %fusion = bf16[64,256]{1,0:T(8,128)(2,1)S(1)} fusion(s32[]{:T(128)S(6)} %select_n.3, bf16[128,128]{1,0:T(8,128)(2,1)} %param.6, bf16[128,128]{1,0:T(8,128)(2,1)} %param.7), kind=kLoop, calls=%fused_computation.9 | loop fusion | flops 65536 | bytes 98308 | tf_op jit(solution)/shard_map/concatenate | solution.py:201
  1.4 5.1 %collective-permute-start.2 = (bf16[64,256]{1,0:T(8,128)(2,1)S(1)}, bf16[64,256]{1,0:T(8,128)(2,1)S(1)}, u32[]{:S(2)}, u32[]{:S(2)}) collective-permute-start(bf16[64,256]{1,0:T(8,128)(2,1)S(1)} %fusion), channel_id=1, source_target_pairs={{0,24},{2,26},{4,28},{6,30},{8,16},{10,18},{12,20},{14,22},{16,8},... | collective-permute-start | bytes 98312 | tf_op jit(solution)/shard_map/ppermute | solution.py:186
  6.5 0.6 %collective-permute-start = (bf16[64,256]{1,0:T(8,128)(2,1)S(1)}, bf16[64,256]{1,0:T(8,128)(2,1)S(1)}, u32[]{:S(2)}, u32[]{:S(2)}) collective-permute-start(bf16[64,256]{1,0:T(8,128)(2,1)S(1)} %fusion), channel_id=1, source_target_pairs={{0,8},{2,10},{4,12},{6,14},{8,0},{10,2},{12,4},{14,6},{16,24},{18,... | collective-permute-start | bytes 98312 | tf_op jit(solution)/shard_map/ppermute | solution.py:186
  7.2 1.3 %collective-permute-done.2 = bf16[64,256]{1,0:T(8,128)(2,1)S(1)} collective-permute-done((bf16[64,256]{1,0:T(8,128)(2,1)S(1)}, bf16[64,256]{1,0:T(8,128)(2,1)S(1)}, u32[]{:S(2)}, u32[]{:S(2)}) %collective-permute-start.2) | collective-permute-done | bytes 32800 | tf_op jit(solution)/shard_map/ppermute | solution.py:186
  8.4 2.9 %collective-permute-done.1 = bf16[64,256]{1,0:T(8,128)(2,1)S(1)} collective-permute-done((bf16[64,256]{1,0:T(8,128)(2,1)S(1)}, bf16[64,256]{1,0:T(8,128)(2,1)S(1)}, u32[]{:S(2)}, u32[]{:S(2)}) %collective-permute-start.1) | collective-permute-done | bytes 32800 | tf_op jit(solution)/shard_map/ppermute | solution.py:186
  11.4 2.5 %collective-permute-start.5 = (bf16[256,256]{1,0:T(8,128)(2,1)S(1)}, bf16[256,256]{1,0:T(8,128)(2,1)S(1)}, u32[]{:S(2)}, u32[]{:S(2)}) collective-permute-start(bf16[256,256]{1,0:T(8,128)(2,1)S(1)} %pad_maximum_fusion.refs_0_), channel_id=1, source_target_pairs={{0,6},{2,4},{4,2},{6,0},{8,14},{10,12},{12,10},{14,8},{16,22},{18,... | collective-permute-start | bytes 393224 | tf_op jit(solution)/shard_map/ppermute | solution.py:186
  14.4 0.5 %collective-permute-start.3 = (bf16[256,256]{1,0:T(8,128)(2,1)S(1)}, bf16[256,256]{1,0:T(8,128)(2,1)S(1)}, u32[]{:S(2)}, u32[]{:S(2)}) collective-permute-start(bf16[256,256]{1,0:T(8,128)(2,1)S(1)} %pad_maximum_fusion.refs_0_), channel_id=1, source_target_pairs={{0,2},{2,0},{4,6},{6,4},{8,10},{10,8},{12,14},{14,12},{16,18},{18,... | collective-permute-start | bytes 393224 | tf_op jit(solution)/shard_map/ppermute | solution.py:186
  14.9 3.8 %collective-permute-done.5.refs_3_ = bf16[256,256]{1,0:T(8,128)(2,1)S(1)} collective-permute-done((bf16[256,256]{1,0:T(8,128)(2,1)S(1)}, bf16[256,256]{1,0:T(8,128)(2,1)S(1)}, u32[]{:S(2)}, u32[]{:S(2)}) %collective-permute-start.5) | collective-permute-done | bytes 131104 | tf_op jit(solution)/shard_map/ppermute | solution.py:186
  18.7 0.8 %collective-permute-done.4.refs_2_ = bf16[256,256]{1,0:T(8,128)(2,1)S(1)} collective-permute-done((bf16[256,256]{1,0:T(8,128)(2,1)S(1)}, bf16[256,256]{1,0:T(8,128)(2,1)S(1)}, u32[]{:S(2)}, u32[]{:S(2)}) %collective-permute-start.4) | collective-permute-done | bytes 131104 | tf_op jit(solution)/shard_map/ppermute | solution.py:186
  19.5 0.5 %collective-permute-start.7 = (bf16[256,256]{1,0:T(8,128)(2,1)S(1)}, bf16[256,256]{1,0:T(8,128)(2,1)S(1)}, u32[]{:S(2)}, u32[]{:S(2)}) collective-permute-start(bf16[256,256]{1,0:T(8,128)(2,1)S(1)} %collective-permute-done.3.refs_1_), channel_id=1, source_target_pairs={{0,1},{1,0},{2,3},{3,2},{4,5},{5,4},{6,7},{7,6},{8,9},{9,8},{10,11... | collective-permute-start | bytes 393224 | tf_op jit(solution)/shard_map/ppermute | solution.py:186
  20.0 0.8 %collective-permute-done.8.refs_6_ = bf16[256,256]{1,0:T(8,128)(2,1)S(1)} collective-permute-done((bf16[256,256]{1,0:T(8,128)(2,1)S(1)}, bf16[256,256]{1,0:T(8,128)(2,1)S(1)}, u32[]{:S(2)}, u32[]{:S(2)}) %collective-permute-start.8) | collective-permute-done | bytes 131104 | tf_op jit(solution)/shard_map/ppermute | solution.py:186
  21.0 0.9 %copy-done.1 = bf16[128,1024]{1,0:T(8,128)(2,1)S(1)} copy-done((bf16[128,1024]{1,0:T(8,128)(2,1)S(1)}, bf16[128,1024]{1,0:T(8,128)(2,1)}, u32[]{:S(2)}) %copy-start.1) | copy-done | bytes 262168
  22.0 7.0 %shard_map.76 = (bf16[128,1024]{1,0:T(8,128)(2,1)}, bf16[256,256]{1,0:T(8,128)(2,1)S(1)}, bf16[256,256]{1,0:T(8,128)(2,1)S(1)}, bf16[256,256]{1,0:T(8,128)(2,1)S...) custom-call(s32[8]{0:T(128)S(1)} %copy-done.2, ...), custom_call_target="tpu_custom_call" | custom-call | tf_op jit(solution)/shard_map/pallas_call | solution.py:163
  30.4 1.1 %collective-permute-start.12 = (bf16[256,256]{1,0:T(8,128)(2,1)S(1)}, bf16[256,256]{1,0:T(8,128)(2,1)S(1)}, u32[]{:S(2)}, u32[]{:S(2)}) collective-permute-start(bf16[256,256]{1,0:T(8,128)(2,1)S(1)} %add_convert_fusion.3), channel_id=1, source_target_pairs={{0,2},{2,0},{4,6},{6,4},{8,10},{10,8},{12,14},{14,12},{16,18},{18,... | collective-permute-start | bytes 393224 | tf_op jit(solution)/shard_map/ppermute | solution.py:186
  31.5 0.9 %collective-permute-start.14 = (bf16[256,256]{1,0:T(8,128)(2,1)S(1)}, bf16[256,256]{1,0:T(8,128)(2,1)S(1)}, u32[]{:S(2)}, u32[]{:S(2)}) collective-permute-start(bf16[256,256]{1,0:T(8,128)(2,1)S(1)} %add_convert_fusion.2), channel_id=1, source_target_pairs={{0,4},{2,6},{4,0},{6,2},{8,12},{10,14},{12,8},{14,10},{16,20},{18,... | collective-permute-start | bytes 393224 | tf_op jit(solution)/shard_map/ppermute | solution.py:186
  32.4 1.7 %collective-permute-start.16 = (bf16[256,256]{1,0:T(8,128)(2,1)S(1)}, bf16[256,256]{1,0:T(8,128)(2,1)S(1)}, u32[]{:S(2)}, u32[]{:S(2)}) collective-permute-start(bf16[256,256]{1,0:T(8,128)(2,1)S(1)} %add_convert_fusion.1), channel_id=1, source_target_pairs={{0,6},{2,4},{4,2},{6,0},{8,14},{10,12},{12,10},{14,8},{16,22},{18,... | collective-permute-start | bytes 393224 | tf_op jit(solution)/shard_map/ppermute | solution.py:186
  34.1 2.6 %collective-permute-done.12 = bf16[256,256]{1,0:T(8,128)(2,1)S(1)} collective-permute-done((bf16[256,256]{1,0:T(8,128)(2,1)S(1)}, bf16[256,256]{1,0:T(8,128)(2,1)S(1)}, u32[]{:S(2)}, u32[]{:S(2)}) %collective-permute-start.12) | collective-permute-done | bytes 131104 | tf_op jit(solution)/shard_map/ppermute | solution.py:186
  36.7 3.1 %collective-permute-done.14 = bf16[256,256]{1,0:T(8,128)(2,1)S(1)} collective-permute-done((bf16[256,256]{1,0:T(8,128)(2,1)S(1)}, bf16[256,256]{1,0:T(8,128)(2,1)S(1)}, u32[]{:S(2)}, u32[]{:S(2)}) %collective-permute-start.14) | collective-permute-done | bytes 131104 | tf_op jit(solution)/shard_map/ppermute | solution.py:186
  40.0 2.7 %collective-permute-start.19 = (bf16[64,256]{1,0:T(8,128)(2,1)S(1)}, bf16[64,256]{1,0:T(8,128)(2,1)S(1)}, u32[]{:S(2)}, u32[]{:S(2)}) collective-permute-start(bf16[64,256]{1,0:T(8,128)(2,1)S(1)} %get-tuple-element.22), channel_id=1, source_target_pairs={{0,24},{2,26},{4,28},{6,30},{8,16},{10,18},{12,20},{14,22},{16,8},... | collective-permute-start | bytes 98312 | tf_op jit(solution)/shard_map/ppermute | solution.py:186
  42.6 0.8 %collective-permute-start.18 = (bf16[64,256]{1,0:T(8,128)(2,1)S(1)}, bf16[64,256]{1,0:T(8,128)(2,1)S(1)}, u32[]{:S(2)}, u32[]{:S(2)}) collective-permute-start(bf16[64,256]{1,0:T(8,128)(2,1)S(1)} %get-tuple-element.23), channel_id=1, source_target_pairs={{0,16},{2,18},{4,20},{6,22},{8,24},{10,26},{12,28},{14,30},{16,0},... | collective-permute-start | bytes 98312 | tf_op jit(solution)/shard_map/ppermute | solution.py:186
  43.5 0.7 %collective-permute-done.17 = bf16[64,256]{1,0:T(8,128)(2,1)S(1)} collective-permute-done((bf16[64,256]{1,0:T(8,128)(2,1)S(1)}, bf16[64,256]{1,0:T(8,128)(2,1)S(1)}, u32[]{:S(2)}, u32[]{:S(2)}) %collective-permute-start.17) | collective-permute-done | bytes 32800 | tf_op jit(solution)/shard_map/ppermute | solution.py:186
  44.1 1.7 %collective-permute-done.19 = bf16[64,256]{1,0:T(8,128)(2,1)S(1)} collective-permute-done((bf16[64,256]{1,0:T(8,128)(2,1)S(1)}, bf16[64,256]{1,0:T(8,128)(2,1)S(1)}, u32[]{:S(2)}, u32[]{:S(2)}) %collective-permute-start.19) | collective-permute-done | bytes 32800 | tf_op jit(solution)/shard_map/ppermute | solution.py:186
  45.8 1.6 %collective-permute-done.18 = bf16[64,256]{1,0:T(8,128)(2,1)S(1)} collective-permute-done((bf16[64,256]{1,0:T(8,128)(2,1)S(1)}, bf16[64,256]{1,0:T(8,128)(2,1)S(1)}, u32[]{:S(2)}, u32[]{:S(2)}) %collective-permute-start.18) | collective-permute-done | bytes 32800 | tf_op jit(solution)/shard_map/ppermute | solution.py:186
  47.5 0.6 %fusion.2 = (bf16[64,128]{1,0:T(8,128)(2,1)}, bf16[64,128]{1,0:T(8,128)(2,1)}) fusion(bf16[64,256]{1,0:T(8,128)(2,1)S(1)} %add_convert_fusion.5), kind=kLoop, calls=%fused_computation.11 | loop fusion | bytes 65536 | tf_op jit(solution)/shard_map/slice | solution.py:227
  (32 shorter events, 2.4 us)
Async XLA Ops:
  0.6 20.4 %copy-start = (bf16[128,1024]{1,0:T(8,128)(2,1)S(1)}, bf16[128,1024]{1,0:T(8,128)(2,1)}, u32[]{:S(2)}) copy-start(bf16[128,1024]{1,0:T(8,128)(2,1)} %q_ref.1) | copy-start | bytes 786436
  1.4 19.6 %copy-start.2 = (s32[8]{0:T(128)S(1)}, s32[8]{0:T(128)}, u32[]{:S(2)}) copy-start(s32[8]{0:T(128)} %lengths_ref.1) | copy-start | bytes 100
  1.4 7.0 %collective-permute-start.2 = (bf16[64,256]{1,0:T(8,128)(2,1)S(1)}, bf16[64,256]{1,0:T(8,128)(2,1)S(1)}, u32[]{:S(2)}, u32[]{:S(2)}) collective-permute-start(bf16[64,256]{1,0:T(8,128)(2,1)S(1)} %fusion), channel_id=1, source_target_pairs={{0,24},{2,26},{4,28},{6,30},{8,16},{10,18},{12,20},{14,22},{16,8},... | collective-permute-start | bytes 98312 | tf_op jit(solution)/shard_map/ppermute | solution.py:186
  6.5 4.8 %collective-permute-start.1 = (bf16[64,256]{1,0:T(8,128)(2,1)S(1)}, bf16[64,256]{1,0:T(8,128)(2,1)S(1)}, u32[]{:S(2)}, u32[]{:S(2)}) collective-permute-start(bf16[64,256]{1,0:T(8,128)(2,1)S(1)} %fusion), channel_id=1, source_target_pairs={{0,16},{2,18},{4,20},{6,22},{8,24},{10,26},{12,28},{14,30},{16,0},... | collective-permute-start | bytes 98312 | tf_op jit(solution)/shard_map/ppermute | solution.py:186
  6.5 4.8 %collective-permute-start = (bf16[64,256]{1,0:T(8,128)(2,1)S(1)}, bf16[64,256]{1,0:T(8,128)(2,1)S(1)}, u32[]{:S(2)}, u32[]{:S(2)}) collective-permute-start(bf16[64,256]{1,0:T(8,128)(2,1)S(1)} %fusion), channel_id=1, source_target_pairs={{0,8},{2,10},{4,12},{6,14},{8,0},{10,2},{12,4},{14,6},{16,24},{18,... | collective-permute-start | bytes 98312 | tf_op jit(solution)/shard_map/ppermute | solution.py:186
  11.4 7.3 %collective-permute-start.5 = (bf16[256,256]{1,0:T(8,128)(2,1)S(1)}, bf16[256,256]{1,0:T(8,128)(2,1)S(1)}, u32[]{:S(2)}, u32[]{:S(2)}) collective-permute-start(bf16[256,256]{1,0:T(8,128)(2,1)S(1)} %pad_maximum_fusion.refs_0_), channel_id=1, source_target_pairs={{0,6},{2,4},{4,2},{6,0},{8,14},{10,12},{12,10},{14,8},{16,22},{18,... | collective-permute-start | bytes 393224 | tf_op jit(solution)/shard_map/ppermute | solution.py:186
  13.9 5.6 %collective-permute-start.4 = (bf16[256,256]{1,0:T(8,128)(2,1)S(1)}, bf16[256,256]{1,0:T(8,128)(2,1)S(1)}, u32[]{:S(2)}, u32[]{:S(2)}) collective-permute-start(bf16[256,256]{1,0:T(8,128)(2,1)S(1)} %pad_maximum_fusion.refs_0_), channel_id=1, source_target_pairs={{0,4},{2,6},{4,0},{6,2},{8,12},{10,14},{12,8},{14,10},{16,20},{18,... | collective-permute-start | bytes 393224 | tf_op jit(solution)/shard_map/ppermute | solution.py:186
  14.4 5.1 %collective-permute-start.3 = (bf16[256,256]{1,0:T(8,128)(2,1)S(1)}, bf16[256,256]{1,0:T(8,128)(2,1)S(1)}, u32[]{:S(2)}, u32[]{:S(2)}) collective-permute-start(bf16[256,256]{1,0:T(8,128)(2,1)S(1)} %pad_maximum_fusion.refs_0_), channel_id=1, source_target_pairs={{0,2},{2,0},{4,6},{6,4},{8,10},{10,8},{12,14},{14,12},{16,18},{18,... | collective-permute-start | bytes 393224 | tf_op jit(solution)/shard_map/ppermute | solution.py:186
  14.9 5.1 %collective-permute-start.6 = (bf16[256,256]{1,0:T(8,128)(2,1)S(1)}, bf16[256,256]{1,0:T(8,128)(2,1)S(1)}, u32[]{:S(2)}, u32[]{:S(2)}) collective-permute-start(bf16[256,256]{1,0:T(8,128)(2,1)S(1)} %pad_maximum_fusion.refs_0_), channel_id=1, source_target_pairs={{0,1},{1,0},{2,3},{3,2},{4,5},{5,4},{6,7},{7,6},{8,9},{9,8},{10,11... | collective-permute-start | bytes 393224 | tf_op jit(solution)/shard_map/ppermute | solution.py:186
  18.7 1.3 %collective-permute-start.9 = (bf16[256,256]{1,0:T(8,128)(2,1)S(1)}, bf16[256,256]{1,0:T(8,128)(2,1)S(1)}, u32[]{:S(2)}, u32[]{:S(2)}) collective-permute-start(bf16[256,256]{1,0:T(8,128)(2,1)S(1)} %collective-permute-done.5.refs_3_), channel_id=1, source_target_pairs={{0,1},{1,0},{2,3},{3,2},{4,5},{5,4},{6,7},{7,6},{8,9},{9,8},{10,11... | collective-permute-start | bytes 393224 | tf_op jit(solution)/shard_map/ppermute | solution.py:186
  19.5 1.3 %collective-permute-start.8 = (bf16[256,256]{1,0:T(8,128)(2,1)S(1)}, bf16[256,256]{1,0:T(8,128)(2,1)S(1)}, u32[]{:S(2)}, u32[]{:S(2)}) collective-permute-start(bf16[256,256]{1,0:T(8,128)(2,1)S(1)} %collective-permute-done.4.refs_2_), channel_id=1, source_target_pairs={{0,1},{1,0},{2,3},{3,2},{4,5},{5,4},{6,7},{7,6},{8,9},{9,8},{10,11... | collective-permute-start | bytes 393224 | tf_op jit(solution)/shard_map/ppermute | solution.py:186
  19.5 1.5 %collective-permute-start.7 = (bf16[256,256]{1,0:T(8,128)(2,1)S(1)}, bf16[256,256]{1,0:T(8,128)(2,1)S(1)}, u32[]{:S(2)}, u32[]{:S(2)}) collective-permute-start(bf16[256,256]{1,0:T(8,128)(2,1)S(1)} %collective-permute-done.3.refs_1_), channel_id=1, source_target_pairs={{0,1},{1,0},{2,3},{3,2},{4,5},{5,4},{6,7},{7,6},{8,9},{9,8},{10,11... | collective-permute-start | bytes 393224 | tf_op jit(solution)/shard_map/ppermute | solution.py:186
  21.0 1.0 %copy-start.1 = (bf16[128,1024]{1,0:T(8,128)(2,1)S(1)}, bf16[128,1024]{1,0:T(8,128)(2,1)}, u32[]{:S(2)}) copy-start(bf16[128,1024]{1,0:T(8,128)(2,1)} %g_ref.1) | copy-start | bytes 786436
  29.0 1.3 %collective-permute-start.11 = (bf16[256,256]{1,0:T(8,128)(2,1)S(1)}, bf16[256,256]{1,0:T(8,128)(2,1)S(1)}, u32[]{:S(2)}, u32[]{:S(2)}) collective-permute-start(bf16[256,256]{1,0:T(8,128)(2,1)S(1)} %get-tuple-element.16), channel_id=1, source_target_pairs={{0,1},{1,0},{2,3},{3,2},{4,5},{5,4},{6,7},{7,6},{8,9},{9,8},{10,11... | collective-permute-start | bytes 393224 | tf_op jit(solution)/shard_map/ppermute | solution.py:186
  29.3 4.8 %collective-permute-start.10 = (bf16[256,256]{1,0:T(8,128)(2,1)S(1)}, bf16[256,256]{1,0:T(8,128)(2,1)S(1)}, u32[]{:S(2)}, u32[]{:S(2)}) collective-permute-start(bf16[256,256]{1,0:T(8,128)(2,1)S(1)} %get-tuple-element.14), channel_id=1, source_target_pairs={{0,1},{1,0},{2,3},{3,2},{4,5},{5,4},{6,7},{7,6},{8,9},{9,8},{10,11... | collective-permute-start | bytes 393224 | tf_op jit(solution)/shard_map/ppermute | solution.py:186
  29.5 2.0 %collective-permute-start.13 = (bf16[256,256]{1,0:T(8,128)(2,1)S(1)}, bf16[256,256]{1,0:T(8,128)(2,1)S(1)}, u32[]{:S(2)}, u32[]{:S(2)}) collective-permute-start(bf16[256,256]{1,0:T(8,128)(2,1)S(1)} %get-tuple-element.18), channel_id=1, source_target_pairs={{0,1},{1,0},{2,3},{3,2},{4,5},{5,4},{6,7},{7,6},{8,9},{9,8},{10,11... | collective-permute-start | bytes 393224 | tf_op jit(solution)/shard_map/ppermute | solution.py:186
  29.8 2.5 %collective-permute-start.15 = (bf16[256,256]{1,0:T(8,128)(2,1)S(1)}, bf16[256,256]{1,0:T(8,128)(2,1)S(1)}, u32[]{:S(2)}, u32[]{:S(2)}) collective-permute-start(bf16[256,256]{1,0:T(8,128)(2,1)S(1)} %get-tuple-element.20), channel_id=1, source_target_pairs={{0,1},{1,0},{2,3},{3,2},{4,5},{5,4},{6,7},{7,6},{8,9},{9,8},{10,11... | collective-permute-start | bytes 393224 | tf_op jit(solution)/shard_map/ppermute | solution.py:186
  30.4 6.4 %collective-permute-start.12 = (bf16[256,256]{1,0:T(8,128)(2,1)S(1)}, bf16[256,256]{1,0:T(8,128)(2,1)S(1)}, u32[]{:S(2)}, u32[]{:S(2)}) collective-permute-start(bf16[256,256]{1,0:T(8,128)(2,1)S(1)} %add_convert_fusion.3), channel_id=1, source_target_pairs={{0,2},{2,0},{4,6},{6,4},{8,10},{10,8},{12,14},{14,12},{16,18},{18,... | collective-permute-start | bytes 393224 | tf_op jit(solution)/shard_map/ppermute | solution.py:186
  31.5 8.3 %collective-permute-start.14 = (bf16[256,256]{1,0:T(8,128)(2,1)S(1)}, bf16[256,256]{1,0:T(8,128)(2,1)S(1)}, u32[]{:S(2)}, u32[]{:S(2)}) collective-permute-start(bf16[256,256]{1,0:T(8,128)(2,1)S(1)} %add_convert_fusion.2), channel_id=1, source_target_pairs={{0,4},{2,6},{4,0},{6,2},{8,12},{10,14},{12,8},{14,10},{16,20},{18,... | collective-permute-start | bytes 393224 | tf_op jit(solution)/shard_map/ppermute | solution.py:186
  32.4 7.4 %collective-permute-start.16 = (bf16[256,256]{1,0:T(8,128)(2,1)S(1)}, bf16[256,256]{1,0:T(8,128)(2,1)S(1)}, u32[]{:S(2)}, u32[]{:S(2)}) collective-permute-start(bf16[256,256]{1,0:T(8,128)(2,1)S(1)} %add_convert_fusion.1), channel_id=1, source_target_pairs={{0,6},{2,4},{4,2},{6,0},{8,14},{10,12},{12,10},{14,8},{16,22},{18,... | collective-permute-start | bytes 393224 | tf_op jit(solution)/shard_map/ppermute | solution.py:186
  39.9 4.2 %collective-permute-start.17 = (bf16[64,256]{1,0:T(8,128)(2,1)S(1)}, bf16[64,256]{1,0:T(8,128)(2,1)S(1)}, u32[]{:S(2)}, u32[]{:S(2)}) collective-permute-start(bf16[64,256]{1,0:T(8,128)(2,1)S(1)} %get-tuple-element.21), channel_id=1, source_target_pairs={{0,8},{2,10},{4,12},{6,14},{8,0},{10,2},{12,4},{14,6},{16,24},{18,... | collective-permute-start | bytes 98312 | tf_op jit(solution)/shard_map/ppermute | solution.py:186
  40.0 5.8 %collective-permute-start.19 = (bf16[64,256]{1,0:T(8,128)(2,1)S(1)}, bf16[64,256]{1,0:T(8,128)(2,1)S(1)}, u32[]{:S(2)}, u32[]{:S(2)}) collective-permute-start(bf16[64,256]{1,0:T(8,128)(2,1)S(1)} %get-tuple-element.22), channel_id=1, source_target_pairs={{0,24},{2,26},{4,28},{6,30},{8,16},{10,18},{12,20},{14,22},{16,8},... | collective-permute-start | bytes 98312 | tf_op jit(solution)/shard_map/ppermute | solution.py:186
  42.6 4.8 %collective-permute-start.18 = (bf16[64,256]{1,0:T(8,128)(2,1)S(1)}, bf16[64,256]{1,0:T(8,128)(2,1)S(1)}, u32[]{:S(2)}, u32[]{:S(2)}) collective-permute-start(bf16[64,256]{1,0:T(8,128)(2,1)S(1)} %get-tuple-element.23), channel_id=1, source_target_pairs={{0,16},{2,18},{4,20},{6,22},{8,24},{10,26},{12,28},{14,30},{16,0},... | collective-permute-start | bytes 98312 | tf_op jit(solution)/shard_map/ppermute | solution.py:186

commit v3 on v2

--- a/solution.py
+++ b/solution.py
@@ -29,12 +29,11 @@
     *refs,
 ):
     outer = ctx_count // inner
-    piece_count = dp_count * inner
-    kv_refs = refs[:piece_count]
-    dq_ref = refs[piece_count]
-    dkv_refs = refs[piece_count + 1 : 2 * piece_count + 1]
+    kv_refs = refs[:dp_count]
+    dq_ref = refs[dp_count]
+    dkv_refs = refs[dp_count + 1 : 2 * dp_count + 1]
     ordered_ref, kt_ref, acc_ref, stack_ref, flip_ref, s_ref, dp_ref, dqt_ref = refs[
-        2 * piece_count + 1 :
+        2 * dp_count + 1 :
     ]
     tok_rows, width = q_ref.shape
     part_rows = tok_rows // dp_count
@@ -49,17 +48,12 @@
 
     dp_index = lax.axis_index("dp")
 
-    def blocks():
-        for piece in range(piece_count):
-            for block in range(outer):
-                owner = ctx_index ^ (piece % inner) ^ (block * inner)
-                position = part_position(
-                    owner, dp_index ^ (piece // inner), ctx_count, part_rows, span_rows
-                )
-                yield piece, pl.ds(block * part_rows, part_rows), pl.ds(position, part_rows)
-
-    for piece, here, ordered in blocks():
-        ordered_ref[ordered, :] = kv_refs[piece][here, :]
+    for far in range(dp_count):
+        for owner in range(ctx_count):
+            position = part_position(owner, dp_index ^ far, ctx_count, part_rows, span_rows)
+            ordered_ref[pl.ds(position, part_rows), :] = kv_refs[far][
+                pl.ds(owner * part_rows, part_rows), :
+            ]
     for part in range(seq // tile):
         rows = pl.ds(part * tile, tile)
         kt_ref[:, rows] = ordered_ref[rows, :head_width].T
@@ -144,11 +138,19 @@
                 head * span_rows : (head + 1) * span_rows
             ]
 
-    for piece, here, ordered in blocks():
-        dkv_refs[piece][here, :head_width] = (scale * acc_ref[ordered, :head_width]).astype(
-            jnp.bfloat16
-        )
-        dkv_refs[piece][here, head_width:] = acc_ref[ordered, head_width:].astype(jnp.bfloat16)
+    for far in range(dp_count):
+        for offset in range(inner):
+            for block in range(outer):
+                here = pl.ds((offset * outer + block) * part_rows, part_rows)
+                owner = ctx_index ^ offset ^ (block * inner)
+                position = part_position(owner, dp_index ^ far, ctx_count, part_rows, span_rows)
+                ordered = pl.ds(position, part_rows)
+                dkv_refs[far][here, :head_width] = (scale * acc_ref[ordered, :head_width]).astype(
+                    jnp.bfloat16
+                )
+                dkv_refs[far][here, head_width:] = acc_ref[ordered, head_width:].astype(
+                    jnp.bfloat16
+                )
 
 
 def attend(ctx_count, dp_count, inner, doc_lengths, queries, out_grads, pieces):
@@ -163,9 +165,9 @@
     results = pl.pallas_call(
         functools.partial(attend_kernel, ctx_count, dp_count, inner, tile),
         out_shape=[jax.ShapeDtypeStruct((tok_rows, width), jnp.bfloat16)]
-        + [jax.ShapeDtypeStruct(piece.shape, jnp.bfloat16) for piece in pieces],
+        + [jax.ShapeDtypeStruct((seq // dp_count, kv_width), jnp.bfloat16)] * dp_count,
         in_specs=[pl.BlockSpec(memory_space=pltpu.SMEM)] + [vmem] * (2 + len(pieces)),
-        out_specs=[vmem] * (1 + len(pieces)),
+        out_specs=[vmem] * (1 + dp_count),
         scratch_shapes=[
             pltpu.VMEM((seq, kv_width), jnp.bfloat16),
             pltpu.VMEM((head_width, seq), jnp.bfloat16),
@@ -200,23 +202,16 @@
     own = lax.dynamic_slice_in_dim(
         jnp.concatenate([keys, values], axis=1), lax.axis_index("dp") * part_rows, part_rows, 0
     )
-    line = jnp.concatenate(
-        [own] + [swap(own, "ctx", block * inner) for block in range(1, outer)], axis=0
-    )
-    plane = [line] + [swap(line, "ctx", offset) for offset in range(1, inner)]
-    pieces = plane + [
-        swap(piece, "dp", offset) for offset in range(1, dp_count) for piece in plane
-    ]
+    half = lax.all_gather(own, "ctx", axis=0, tiled=True)
+    pieces = [half] + [swap(half, "dp", offset) for offset in range(1, dp_count)]
     query_grads, parts = attend(
         ctx_count, dp_count, inner, doc_lengths, queries, out_grads, pieces
     )
-    plane_sums = [
-        total_of(
-            [parts[offset]]
-            + [swap(parts[far * inner + offset], "dp", far) for far in range(1, dp_count)]
-        ).astype(jnp.bfloat16)
-        for offset in range(inner)
-    ]
+    chip_sum = total_of(
+        [parts[0]] + [swap(parts[far], "dp", far) for far in range(1, dp_count)]
+    ).astype(jnp.bfloat16)
+    rows = ctx_count * part_rows // inner
+    plane_sums = [chip_sum[offset * rows : (offset + 1) * rows] for offset in range(inner)]
     line_sum = total_of(
         [plane_sums[0]] + [swap(plane_sums[offset], "ctx", offset) for offset in range(1, inner)]
     ).astype(jnp.bfloat16)

time: 48.6 us -> 74.9 us (1.54)
  blocking collectives: 0 us -> 45.5 us
  starting transfers between devices: 18.1 us -> 7.2 us
  waiting for transfers between devices: 19.7 us -> 12.6 us
  local copies, waits for them, and re-layouts: 1.58 us -> 0.67 us
    all_gather x0 -> x1, blocking collectives: none -> 45.5 us  [body(): half = lax.all_gather(own, 'ctx', axis=0, tiled=True)]
    ppermute x20 -> x8, starting transfers between devices: 18.1 us -> 7.2 us  [swap(): return lax.ppermute(value, axis, pairs)]
    ppermute x20 -> x8, waiting for transfers between devices: 19.7 us -> 12.6 us  [swap(): return lax.ppermute(value, axis, pairs)]
    unnamed x6, local copies, waits for them, and re-layouts: 0.96 us -> 0.01 us
  transfers between devices with their start and end apart: 20 -> 8, of which waited for: 13 -> 8; matrix products, arithmetic and copies ran while one was open for 0% -> 0% of each run, Pallas kernels for 0% -> 0%
where the time goes in v3:
time: 74.9 us; the launch traced here: 74.7 us
  blocking collectives  45.5 us (61%)
  waiting for transfers between devices  12.6 us (17%)
  starting transfers between devices  7.2 us (10%)
  Pallas kernels  7.01 us (9%)
  other arithmetic  0.99 us (1%)
    all_gather x1, blocking collectives, body(): half = lax.all_gather(own, 'ctx', axis=0, tiled=True)  45.5 us
    ppermute x8, waiting for transfers between devices, swap(): return lax.ppermute(value, axis, pairs)  12.6 us
    ppermute x8, starting transfers between devices, swap(): return lax.ppermute(value, axis, pairs)  7.2 us
    pallas_call x1, Pallas kernels, attend(): pl.pallas_call(functools.partial(attend_kernel, ctx_count, dp_count, inne...  7.01 us
  transfers between devices with their start and end apart: 8, of which 8 were waited for; matrix products, arithmetic and copies ran while one was open for 0% of the time, Pallas kernels for 0%

profile of v3, /device:TPU:0, one launch (start us, length us, event | category | flops | bytes accessed | tf_op | source)
XLA Modules:
  0.0 74.7 jit_solution(451357509579686789)
XLA Ops:
  0.6 0.7 fusion
  1.4 0.0 copy-start.2
  1.4 45.5 %all_gather.3.refs_0_ = bf16[1024,256]{1,0:T(8,128)(2,1)S(1)} all-gather(bf16[64,256]{1,0:T(8,128)(2,1)S(1)} %fusion), channel_id=1, replica_groups=mesh['ctx'=16,'dp'=2] {'ctx'}, dimensions={0}, use_global_device_ids=true | all-gather | bytes 557056 | tf_op jit(solution)/shard_map/all_gather | solution.py:205
  46.9 0.0 collective-permute-start
  46.9 1.9 %collective-permute-done.refs_1_ = bf16[1024,256]{1,0:T(8,128)(2,1)S(1)} collective-permute-done((bf16[1024,256]{1,0:T(8,128)(2,1)S(1)}, bf16[1024,256]{1,0:T(8,128)(2,1)S(1)}, u32[]{:S(2)}, u32[]{:S(2)}) %collective-permute-start) | collective-permute-done | bytes 524320 | tf_op jit(solution)/shard_map/ppermute | solution.py:188
  48.8 0.0 copy-done.2
  48.8 7.0 %shard_map.76 = (bf16[128,1024]{1,0:T(8,128)(2,1)}, bf16[1024,256]{1,0:T(8,128)(2,1)S(1)}, bf16[1024,256]{1,0:T(8,128)(2,1)S(1)}) custom-call(s32[8]{0:T(128)S(1)} %copy-done.2, bf16[128,1024]{1,0:T(8,128)(2,1)S(1)} %copy-done, bf16[128,1024]{1,0:T(8,128)(2,1)S(1)} %copy-done.1, bf16[1024,256]{1,0:T(8,128)(2,1)S(1)} %all_gather.3.refs_0_, ...), custom_call_target="tpu_custom_call" | custom-call | tf_op jit(solution)/shard_map/pallas_call | solution.py:165
  55.8 0.1 collective-permute-start.1
  55.9 1.8 %collective-permute-done.1 = bf16[1024,256]{1,0:T(8,128)(2,1)S(1)} collective-permute-done((bf16[1024,256]{1,0:T(8,128)(2,1)S(1)}, bf16[1024,256]{1,0:T(8,128)(2,1)S(1)}, u32[]{:S(2)}, u32[]{:S(2)}) %collective-permute-start.1) | collective-permute-done | bytes 524320 | tf_op jit(solution)/shard_map/ppermute | solution.py:188
  57.7 0.1 add_convert_fusion
  57.9 0.1 collective-permute-start.2
  58.0 0.1 collective-permute-start.4
  58.1 3.4 %collective-permute-start.3 = (bf16[256,256]{1,0:T(8,128)(2,1)S(1)}, bf16[256,256]{1,0:T(8,128)(2,1)S(1)}, u32[]{:S(2)}, u32[]{:S(2)}) collective-permute-start(bf16[256,256]{1,0:T(8,128)(2,1)S(1)} %get-tuple-element.11), channel_id=1, source_target_pairs={{0,4},{2,6},{4,0},{6,2},{8,12},{10,14},{12,8},{14,10},{16,20},{18,... | collective-permute-start | bytes 393224 | tf_op jit(solution)/shard_map/ppermute | solution.py:188
  61.5 2.9 %collective-permute-done.2 = bf16[256,256]{1,0:T(8,128)(2,1)S(1)} collective-permute-done((bf16[256,256]{1,0:T(8,128)(2,1)S(1)}, bf16[256,256]{1,0:T(8,128)(2,1)S(1)}, u32[]{:S(2)}, u32[]{:S(2)}) %collective-permute-start.2) | collective-permute-done | bytes 131104 | tf_op jit(solution)/shard_map/ppermute | solution.py:188
  64.3 0.3 collective-permute-done.4
  64.6 2.7 %collective-permute-done.3 = bf16[256,256]{1,0:T(8,128)(2,1)S(1)} collective-permute-done((bf16[256,256]{1,0:T(8,128)(2,1)S(1)}, bf16[256,256]{1,0:T(8,128)(2,1)S(1)}, u32[]{:S(2)}, u32[]{:S(2)}) %collective-permute-start.3) | collective-permute-done | bytes 131104 | tf_op jit(solution)/shard_map/ppermute | solution.py:188
  67.3 0.1 add_convert_fusion.1
  67.4 0.1 collective-permute-start.5
  67.5 0.1 collective-permute-start.7
  67.5 3.4 %collective-permute-start.6 = (bf16[64,256]{1,0:T(8,128)(2,1)S(1)}, bf16[64,256]{1,0:T(8,128)(2,1)S(1)}, u32[]{:S(2)}, u32[]{:S(2)}) collective-permute-start(bf16[64,256]{1,0:T(8,128)(2,1)S(1)} %get-tuple-element.14), channel_id=1, source_target_pairs={{0,16},{2,18},{4,20},{6,22},{8,24},{10,26},{12,28},{14,30},{16,0},... | collective-permute-start | bytes 98312 | tf_op jit(solution)/shard_map/ppermute | solution.py:188
  70.9 0.4 collective-permute-done.5
  71.4 1.9 %collective-permute-done.7 = bf16[64,256]{1,0:T(8,128)(2,1)S(1)} collective-permute-done((bf16[64,256]{1,0:T(8,128)(2,1)S(1)}, bf16[64,256]{1,0:T(8,128)(2,1)S(1)}, u32[]{:S(2)}, u32[]{:S(2)}) %collective-permute-start.7) | collective-permute-done | bytes 32800 | tf_op jit(solution)/shard_map/ppermute | solution.py:188
  73.3 0.8 %collective-permute-done.6 = bf16[64,256]{1,0:T(8,128)(2,1)S(1)} collective-permute-done((bf16[64,256]{1,0:T(8,128)(2,1)S(1)}, bf16[64,256]{1,0:T(8,128)(2,1)S(1)}, u32[]{:S(2)}, u32[]{:S(2)}) %collective-permute-start.6) | collective-permute-done | bytes 32800 | tf_op jit(solution)/shard_map/ppermute | solution.py:188
  74.1 0.6 fusion.3
  (7 shorter events, 0.1 us)
Async XLA Ops:
  1.4 47.4 %copy-start = (bf16[128,1024]{1,0:T(8,128)(2,1)S(1)}, bf16[128,1024]{1,0:T(8,128)(2,1)}, u32[]{:S(2)}) copy-start(bf16[128,1024]{1,0:T(8,128)(2,1)} %q_ref.1) | copy-start | bytes 786436
  1.4 47.4 %copy-start.1 = (bf16[128,1024]{1,0:T(8,128)(2,1)S(1)}, bf16[128,1024]{1,0:T(8,128)(2,1)}, u32[]{:S(2)}) copy-start(bf16[128,1024]{1,0:T(8,128)(2,1)} %g_ref.1) | copy-start | bytes 786436
  1.4 47.4 %copy-start.2 = (s32[8]{0:T(128)S(1)}, s32[8]{0:T(128)}, u32[]{:S(2)}) copy-start(s32[8]{0:T(128)} %lengths_ref.1) | copy-start | bytes 100
  46.9 1.9 %collective-permute-start = (bf16[1024,256]{1,0:T(8,128)(2,1)S(1)}, bf16[1024,256]{1,0:T(8,128)(2,1)S(1)}, u32[]{:S(2)}, u32[]{:S(2)}) collective-permute-start(bf16[1024,256]{1,0:T(8,128)(2,1)S(1)} %all_gather.3.refs_0_), channel_id=1, source_target_pairs={{0,1},{1,0},{2,3},{3,2},{4,5},{5,4},{6,7},{7,6},{8,9},{9,8},{10,11... | collective-permute-start | bytes 1572872 | tf_op jit(solution)/shard_map/ppermute | solution.py:188
  55.8 1.9 %collective-permute-start.1 = (bf16[1024,256]{1,0:T(8,128)(2,1)S(1)}, bf16[1024,256]{1,0:T(8,128)(2,1)S(1)}, u32[]{:S(2)}, u32[]{:S(2)}) collective-permute-start(bf16[1024,256]{1,0:T(8,128)(2,1)S(1)} %get-tuple-element.8), channel_id=1, source_target_pairs={{0,1},{1,0},{2,3},{3,2},{4,5},{5,4},{6,7},{7,6},{8,9},{9,8},{10,11... | collective-permute-start | bytes 1572872 | tf_op jit(solution)/shard_map/ppermute | solution.py:188
  57.9 6.4 %collective-permute-start.2 = (bf16[256,256]{1,0:T(8,128)(2,1)S(1)}, bf16[256,256]{1,0:T(8,128)(2,1)S(1)}, u32[]{:S(2)}, u32[]{:S(2)}) collective-permute-start(bf16[256,256]{1,0:T(8,128)(2,1)S(1)} %get-tuple-element.9), channel_id=1, source_target_pairs={{0,2},{2,0},{4,6},{6,4},{8,10},{10,8},{12,14},{14,12},{16,18},{18,... | collective-permute-start | bytes 393224 | tf_op jit(solution)/shard_map/ppermute | solution.py:188
  58.0 6.6 %collective-permute-start.4 = (bf16[256,256]{1,0:T(8,128)(2,1)S(1)}, bf16[256,256]{1,0:T(8,128)(2,1)S(1)}, u32[]{:S(2)}, u32[]{:S(2)}) collective-permute-start(bf16[256,256]{1,0:T(8,128)(2,1)S(1)} %get-tuple-element.10), channel_id=1, source_target_pairs={{0,6},{2,4},{4,2},{6,0},{8,14},{10,12},{12,10},{14,8},{16,22},{18,... | collective-permute-start | bytes 393224 | tf_op jit(solution)/shard_map/ppermute | solution.py:188
  58.1 9.2 %collective-permute-start.3 = (bf16[256,256]{1,0:T(8,128)(2,1)S(1)}, bf16[256,256]{1,0:T(8,128)(2,1)S(1)}, u32[]{:S(2)}, u32[]{:S(2)}) collective-permute-start(bf16[256,256]{1,0:T(8,128)(2,1)S(1)} %get-tuple-element.11), channel_id=1, source_target_pairs={{0,4},{2,6},{4,0},{6,2},{8,12},{10,14},{12,8},{14,10},{16,20},{18,... | collective-permute-start | bytes 393224 | tf_op jit(solution)/shard_map/ppermute | solution.py:188
  67.4 4.0 %collective-permute-start.5 = (bf16[64,256]{1,0:T(8,128)(2,1)S(1)}, bf16[64,256]{1,0:T(8,128)(2,1)S(1)}, u32[]{:S(2)}, u32[]{:S(2)}) collective-permute-start(bf16[64,256]{1,0:T(8,128)(2,1)S(1)} %get-tuple-element.12), channel_id=1, source_target_pairs={{0,8},{2,10},{4,12},{6,14},{8,0},{10,2},{12,4},{14,6},{16,24},{18,... | collective-permute-start | bytes 98312 | tf_op jit(solution)/shard_map/ppermute | solution.py:188
  67.5 5.8 %collective-permute-start.7 = (bf16[64,256]{1,0:T(8,128)(2,1)S(1)}, bf16[64,256]{1,0:T(8,128)(2,1)S(1)}, u32[]{:S(2)}, u32[]{:S(2)}) collective-permute-start(bf16[64,256]{1,0:T(8,128)(2,1)S(1)} %get-tuple-element.13), channel_id=1, source_target_pairs={{0,24},{2,26},{4,28},{6,30},{8,16},{10,18},{12,20},{14,22},{16,8},... | collective-permute-start | bytes 98312 | tf_op jit(solution)/shard_map/ppermute | solution.py:188
  67.5 6.5 %collective-permute-start.6 = (bf16[64,256]{1,0:T(8,128)(2,1)S(1)}, bf16[64,256]{1,0:T(8,128)(2,1)S(1)}, u32[]{:S(2)}, u32[]{:S(2)}) collective-permute-start(bf16[64,256]{1,0:T(8,128)(2,1)S(1)} %get-tuple-element.14), channel_id=1, source_target_pairs={{0,16},{2,18},{4,20},{6,22},{8,24},{10,26},{12,28},{14,30},{16,0},... | collective-permute-start | bytes 98312 | tf_op jit(solution)/shard_map/ppermute | solution.py:188

commit v4 on v2

v4 whole, which is shorter than its diff:
```python
import functools
import math

import jax
import jax.numpy as jnp
from jax import lax
from jax.experimental import pallas as pl
from jax.experimental.pallas import tpu as pltpu
from jax.sharding import PartitionSpec as P

masked_value = -1e30


def part_position(ctx_index, dp_index, ctx_count, part_rows, span_rows):
    start = dp_index * part_rows
    low = ctx_index * span_rows + start
    high = (2 * ctx_count - 1 - ctx_index) * span_rows + start - span_rows
    return pl.multiple_of(jnp.where(start < span_rows, low, high), part_rows)


def tile_range(half, ctx_index, ctx_count, span_rows, tile, lengths_ref):
    span = ctx_index if half == 0 else 2 * ctx_count - 1 - ctx_index
    first = span * span_rows
    first_key = jnp.int32(0)
    end = jnp.int32(0)
    for doc in range(lengths_ref.shape[0]):
        end = end + lengths_ref[doc]
        first_key = jnp.where(first >= end, end, first_key)
    return first, first_key // tile, (first + span_rows + tile - 1) // tile


def prepare_kernel(q_hbm, g_hbm, line_ref, stack_ref, flip_ref, same_ref, raw_ref, sems):
    tok_rows = q_hbm.shape[0]
    head_width = stack_ref.shape[3]
    span_rows = tok_rows // 2
    copies = [
        pltpu.make_async_copy(source, raw_ref.at[slot], sems.at[slot])
        for slot, source in enumerate((q_hbm, g_hbm))
    ]
    for copy in copies:
        copy.start()
    same_ref[...] = line_ref[...]
    for slot, copy in enumerate(copies):
        copy.wait()
        for half in range(2):
            for head in range(q_hbm.shape[1] // head_width):
                stack_ref[half, slot, pl.ds(head * span_rows, span_rows), :] = raw_ref[
                    slot,
                    pl.ds(half * span_rows, span_rows),
                    pl.ds(head * head_width, head_width),
                ]
            flip_ref[half, slot] = stack_ref[half, slot].T


def attend_kernel(ctx_count, dp_count, inner, tile, lengths_ref, stack_ref, flip_ref, *refs):
    outer = ctx_count // inner
    piece_count = dp_count * inner
    kv_refs = refs[:piece_count]
    keys_ref, dlogits_ref = refs[piece_count : piece_count + 2]
    dkv_refs = refs[piece_count + 2 : 2 * piece_count + 2]
    values_ref, acc_ref, terms_ref, dweights_ref, tops_ref = refs[2 * piece_count + 2 :]
    cols, head_width = stack_ref.shape[2:]
    seq = keys_ref.shape[0]
    tok_rows = seq // ctx_count
    part_rows = tok_rows // dp_count
    span_rows = tok_rows // 2
    scale = head_width ** (-0.5)
    ctx_index = lax.axis_index("ctx")
    dp_index = lax.axis_index("dp")

    def blocks():
        for piece in range(piece_count):
            for block in range(outer):
                owner = ctx_index ^ (piece % inner) ^ (block * inner)
                position = part_position(
                    owner, dp_index ^ (piece // inner), ctx_count, part_rows, span_rows
                )
                yield piece, pl.ds(block * part_rows, part_rows), pl.ds(position, part_rows)

    for piece, here, ordered in blocks():
        keys_ref[ordered, :] = kv_refs[piece][here, :head_width]
        values_ref[ordered, :] = kv_refs[piece][here, head_width:]
    acc_ref[...] = jnp.zeros_like(acc_ref)

    for half in range(2):
        first, tile_low, tile_high = tile_range(
            half, ctx_index, ctx_count, span_rows, tile, lengths_ref
        )
        query_pos = first + lax.rem(
            lax.broadcasted_iota(jnp.int32, (1, cols), 1), jnp.int32(span_rows)
        )
        doc_start = jnp.zeros((1, cols), jnp.int32)
        end = jnp.int32(0)
        for doc in range(lengths_ref.shape[0]):
            end = end + lengths_ref[doc]
            doc_start = jnp.where(query_pos >= end, end, doc_start)

        def sums_step(index, state):
            top, total, mixed = state
            rows = pl.ds(pl.multiple_of(index * tile, tile), tile)
            logits = jnp.dot(
                keys_ref[rows, :], flip_ref[half, 0], preferred_element_type=jnp.float32
            )
            key_pos = lax.broadcasted_iota(jnp.int32, (tile, cols), 0)
            live = (key_pos >= doc_start - index * tile) & (key_pos <= query_pos - index * tile)
            logits = jnp.where(live, logits * (scale * math.log2(math.e)), masked_value)
            new_top = jnp.maximum(top, jnp.max(logits, axis=0, keepdims=True))
            terms = jnp.exp2(logits - new_top)
            dweights = jnp.dot(
                values_ref[rows, :], flip_ref[half, 1], preferred_element_type=jnp.float32
            )
            terms_ref[rows, :] = terms
            dweights_ref[rows, :] = dweights
            tops_ref[pl.ds(index, 1), :] = new_top
            decay = jnp.exp2(top - new_top)
            return (
                new_top,
                total * decay + jnp.sum(terms, axis=0, keepdims=True),
                mixed * decay + jnp.sum(terms * dweights, axis=0, keepdims=True),
            )

        zero = jnp.zeros((1, cols), jnp.float32)
        top, total, mixed = lax.fori_loop(
            tile_low, tile_high, sums_step, (jnp.full_like(zero, masked_value), zero, zero)
        )
        inverse = 1.0 / total
        delta = mixed * inverse

        def grads_step(index, carry):
            rows = pl.ds(pl.multiple_of(index * tile, tile), tile)
            factor = jnp.exp2(tops_ref[pl.ds(index, 1), :] - top) * inverse
            weights = terms_ref[rows, :] * factor
            dlogits = (weights * (dweights_ref[rows, :] - delta)).astype(jnp.bfloat16)
            dlogits_ref[half, rows, :] = dlogits
            acc_ref[rows, head_width:] += jnp.dot(
                weights.astype(jnp.bfloat16),
                stack_ref[half, 1],
                preferred_element_type=jnp.float32,
            )
            acc_ref[rows, :head_width] += jnp.dot(
                dlogits, stack_ref[half, 0], preferred_element_type=jnp.float32
            )
            return carry

        lax.fori_loop(tile_low, tile_high, grads_step, 0)

    for piece, here, ordered in blocks():
        dkv_refs[piece][here, :head_width] = (scale * acc_ref[ordered, :head_width]).astype(
            jnp.bfloat16
        )
        dkv_refs[piece][here, head_width:] = acc_ref[ordered, head_width:].astype(jnp.bfloat16)


def query_kernel(ctx_count, tile, lengths_ref, keys_ref, dlogits_ref, order_ref, dq_ref, sum_ref):
    tok_rows = dq_ref.shape[0]
    head_width = keys_ref.shape[1]
    span_rows = tok_rows // 2
    scale = head_width ** (-0.5)
    ctx_index = lax.axis_index("ctx")
    for half in range(2):
        _, tile_low, tile_high = tile_range(
            half, ctx_index, ctx_count, span_rows, tile, lengths_ref
        )
        sum_ref[...] = jnp.zeros_like(sum_ref)

        def query_step(index, carry):
            rows = pl.ds(pl.multiple_of(index * tile, tile), tile)
            sum_ref[...] += jnp.dot(
                keys_ref[rows, :].T, dlogits_ref[half, rows, :], preferred_element_type=jnp.float32
            )
            return carry

        lax.fori_loop(tile_low, tile_high, query_step, 0)
        grads = (scale * sum_ref[...]).T.astype(jnp.bfloat16)
        for head in range(dq_ref.shape[1] // head_width):
            dq_ref[
                pl.ds(half * span_rows, span_rows), pl.ds(head * head_width, head_width)
            ] = grads[head * span_rows : (head + 1) * span_rows]


vmem = pl.BlockSpec(memory_space=pltpu.VMEM)
smem = pl.BlockSpec(memory_space=pltpu.SMEM)


def prepare(queries, out_grads, head_width, line):
    tok_rows, width = queries.shape
    cols = width // head_width * (tok_rows // 2)
    hbm = pl.BlockSpec(memory_space=pltpu.HBM)
    return pl.pallas_call(
        prepare_kernel,
        out_shape=(
            jax.ShapeDtypeStruct((2, 2, cols, head_width), jnp.bfloat16),
            jax.ShapeDtypeStruct((2, 2, head_width, cols), jnp.bfloat16),
            jax.ShapeDtypeStruct(line.shape, line.dtype),
        ),
        in_specs=[hbm, hbm, vmem],
        out_specs=(vmem, vmem, vmem),
        scratch_shapes=[
            pltpu.VMEM((2, tok_rows, width), jnp.bfloat16),
            pltpu.SemaphoreType.DMA((2,)),
        ],
        compiler_params=pltpu.CompilerParams(vmem_limit_bytes=4 * 1024 * 1024),
    )(queries, out_grads, line)


def attend(ctx_count, dp_count, inner, tile, doc_lengths, stacked, flipped, pieces):
    cols, head_width = stacked.shape[2:]
    seq = ctx_count * dp_count * pieces[0].shape[0] // (ctx_count // inner)
    results = pl.pallas_call(
        functools.partial(attend_kernel, ctx_count, dp_count, inner, tile),
        out_shape=[
            jax.ShapeDtypeStruct((seq, head_width), jnp.bfloat16),
            jax.ShapeDtypeStruct((2, seq, cols), jnp.bfloat16),
        ]
        + [jax.ShapeDtypeStruct(piece.shape, jnp.bfloat16) for piece in pieces],
        in_specs=[smem] + [vmem] * (2 + len(pieces)),
        out_specs=[vmem] * (2 + len(pieces)),
        scratch_shapes=[
            pltpu.VMEM((seq, head_width), jnp.bfloat16),
            pltpu.VMEM((seq, 2 * head_width), jnp.float32),
            pltpu.VMEM((seq, cols), jnp.float32),
            pltpu.VMEM((seq, cols), jnp.float32),
            pltpu.VMEM((seq // tile, cols), jnp.float32),
        ],
        compiler_params=pltpu.CompilerParams(vmem_limit_bytes=32 * 1024 * 1024),
    )(doc_lengths, stacked, flipped, *pieces)
    return results[0], results[1], results[2:]


def query_side(ctx_count, tile, doc_lengths, keys_ordered, dlogits, order, tok_rows):
    cols = dlogits.shape[2]
    head_width = keys_ordered.shape[1]
    return pl.pallas_call(
        functools.partial(query_kernel, ctx_count, tile),
        out_shape=jax.ShapeDtypeStruct(
            (tok_rows, cols // (tok_rows // 2) * head_width), jnp.bfloat16
        ),
        in_specs=[smem, vmem, vmem, pl.BlockSpec(memory_space=pl.ANY)],
        out_specs=vmem,
        scratch_shapes=[pltpu.VMEM((head_width, cols), jnp.float32)],
        compiler_params=pltpu.CompilerParams(vmem_limit_bytes=8 * 1024 * 1024),
    )(doc_lengths, keys_ordered, dlogits, order)


def swap(value, axis, offset):
    pairs = [(index, index ^ offset) for index in range(lax.axis_size(axis))]
    return lax.ppermute(value, axis, pairs)


def total_of(terms):
    return sum(term.astype(jnp.float32) for term in terms)


def body(queries, keys, values, out_grads, doc_lengths):
    ctx_count = lax.axis_size("ctx")
    dp_count = lax.axis_size("dp")
    inner = math.gcd(4, ctx_count)
    outer = ctx_count // inner
    tok_rows, head_width = keys.shape
    part_rows = tok_rows // dp_count
    own = lax.dynamic_slice_in_dim(
        jnp.concatenate([keys, values], axis=1), lax.axis_index("dp") * part_rows, part_rows, 0
    )
    line = jnp.concatenate(
        [own] + [swap(own, "ctx", block * inner) for block in range(1, outer)], axis=0
    )
    plane = [line] + [swap(line, "ctx", offset) for offset in range(1, inner)]
    stacked, flipped, line = prepare(queries, out_grads, head_width, line)
    plane[0] = line
    pieces = plane + [
        swap(piece, "dp", offset) for offset in range(1, dp_count) for piece in plane
    ]
    tile = math.gcd(256, ctx_count * tok_rows)
    keys_ordered, dlogits, parts = attend(
        ctx_count, dp_count, inner, tile, doc_lengths, stacked, flipped, pieces
    )
    plane_sums = [
        total_of(
            [parts[offset]]
            + [swap(parts[far * inner + offset], "dp", far) for far in range(1, dp_count)]
        ).astype(jnp.bfloat16)
        for offset in range(inner)
    ]
    query_grads = query_side(
        ctx_count, tile, doc_lengths, keys_ordered, dlogits, plane_sums[-1], tok_rows
    )
    line_sum = total_of(
        [plane_sums[0]] + [swap(plane_sums[offset], "ctx", offset) for offset in range(1, inner)]
    ).astype(jnp.bfloat16)
    blocks = [line_sum[block * part_rows : (block + 1) * part_rows] for block in range(outer)]
    kv_grads = total_of(
        [blocks[0]] + [swap(blocks[block], "ctx", block * inner) for block in range(1, outer)]
    ).astype(jnp.bfloat16)
    return (query_grads, kv_grads[:, :head_width], kv_grads[:, head_width:])


def solution(mesh):
    return jax.shard_map(
        body,
        mesh=mesh,
        in_specs=(P("ctx", "dp"), P("ctx", None), P("ctx", None), P("ctx", "dp"), P()),
        out_specs=(P("ctx", "dp"), P(("ctx", "dp"), None), P(("ctx", "dp"), None)),
        check_vma=False,
    )
```

time: 48.6 us -> 47.1 us (0.969); the launches traced: 48.1 us -> 47.2 us
  waiting for transfers between devices: 19.7 us -> 16.2 us
  starting transfers between devices: 18.1 us -> 21.3 us
  Pallas kernels: 7 us -> 4.79 us
  local copies, waits for them, and re-layouts: 1.58 us -> 3.18 us
    pallas_call x1, Pallas kernels: 7 us -> 2.55 us  [attend(): pl.pallas_call(functools.partial(attend_kernel, ctx_count, dp_count, inne...]
    ppermute x20, waiting for transfers between devices: 19.7 us -> 16.2 us  [swap(): return lax.ppermute(value, axis, pairs)]
    ppermute x20, starting transfers between devices: 18.1 us -> 21.3 us  [swap(): return lax.ppermute(value, axis, pairs)]
    pallas_call x0 -> x2, Pallas kernels: none -> 2.25 us  [the longest x1 1.9 us: query_side(): pl.pallas_call(functools.partial(query_kernel, ctx_count, tile), out_shap...]
    unnamed x6, local copies, waits for them, and re-layouts: 0.96 us -> 2.55 us
  transfers between devices with their start and end apart: 20 -> 20, of which waited for: 13 -> 11; matrix products, arithmetic and copies ran while one was open for 0% -> 0% of each run, Pallas kernels for 0% -> 5%
where the time goes in v4:
time: 47.1 us; the launch traced here: 47.2 us
  starting transfers between devices  21.3 us (45%)
  waiting for transfers between devices  16.2 us (34%)
  Pallas kernels  4.79 us (10%)
  local copies, waits for them, and re-layouts  3.18 us (7%)
  other arithmetic  0.96 us (2%)
  between operations  0.71 us (2%)
    ppermute x20, starting transfers between devices, swap(): return lax.ppermute(value, axis, pairs)  21.3 us
    ppermute x20, waiting for transfers between devices, swap(): return lax.ppermute(value, axis, pairs)  16.2 us
    unnamed x6, local copies, waits for them, and re-layouts  2.55 us
    pallas_call x1, Pallas kernels, attend(): pl.pallas_call(functools.partial(attend_kernel, ctx_count, dp_count, inne...  2.55 us
    pallas_call x1, Pallas kernels, query_side(): pl.pallas_call(functools.partial(query_kernel, ctx_count, tile), out_shap...  1.9 us
  transfers between devices with their start and end apart: 20, of which 11 were waited for; matrix products, arithmetic and copies ran while one was open for 0% of the time, Pallas kernels for 5%

profile of v4, /device:TPU:0, one launch (start us, length us, event | category | flops | bytes accessed | tf_op | source)
XLA Modules:
  0.0 47.2 jit_solution(11147001089229100397)
XLA Ops:
  0.6 0.7 %fusion = bf16[64,256]{1,0:T(8,128)(2,1)S(1)} fusion(s32[]{:T(128)S(6)} %select_n.3, bf16[128,128]{1,0:T(8,128)(2,1)} %param.6, bf16[128,128]{1,0:T(8,128)(2,1)} %param.7), kind=kLoop, calls=%fused_computation.9 | loop fusion | flops 65536 | bytes 98308 | tf_op jit(solution)/shard_map/concatenate | solution.py:262
  1.4 5.0 %collective-permute-start.2 = (bf16[64,256]{1,0:T(8,128)(2,1)S(1)}, bf16[64,256]{1,0:T(8,128)(2,1)S(1)}, u32[]{:S(2)}, u32[]{:S(2)}) collective-permute-start(bf16[64,256]{1,0:T(8,128)(2,1)S(1)} %fusion), channel_id=1, source_target_pairs={{0,24},{2,26},{4,28},{6,30},{8,16},{10,18},{12,20},{14,22},{16,8},... | collective-permute-start | bytes 98312 | tf_op jit(solution)/shard_map/ppermute | solution.py:247
  6.4 0.6 %collective-permute-start = (bf16[64,256]{1,0:T(8,128)(2,1)S(1)}, bf16[64,256]{1,0:T(8,128)(2,1)S(1)}, u32[]{:S(2)}, u32[]{:S(2)}) collective-permute-start(bf16[64,256]{1,0:T(8,128)(2,1)S(1)} %fusion), channel_id=1, source_target_pairs={{0,8},{2,10},{4,12},{6,14},{8,0},{10,2},{12,4},{14,6},{16,24},{18,... | collective-permute-start | bytes 98312 | tf_op jit(solution)/shard_map/ppermute | solution.py:247
  7.1 1.3 %collective-permute-done.2 = bf16[64,256]{1,0:T(8,128)(2,1)S(1)} collective-permute-done((bf16[64,256]{1,0:T(8,128)(2,1)S(1)}, bf16[64,256]{1,0:T(8,128)(2,1)S(1)}, u32[]{:S(2)}, u32[]{:S(2)}) %collective-permute-start.2) | collective-permute-done | bytes 32800 | tf_op jit(solution)/shard_map/ppermute | solution.py:247
  8.3 2.9 %collective-permute-done.1 = bf16[64,256]{1,0:T(8,128)(2,1)S(1)} collective-permute-done((bf16[64,256]{1,0:T(8,128)(2,1)S(1)}, bf16[64,256]{1,0:T(8,128)(2,1)S(1)}, u32[]{:S(2)}, u32[]{:S(2)}) %collective-permute-start.1) | collective-permute-done | bytes 32800 | tf_op jit(solution)/shard_map/ppermute | solution.py:247
  11.3 2.5 %collective-permute-start.5 = (bf16[256,256]{1,0:T(8,128)(2,1)S(1)}, bf16[256,256]{1,0:T(8,128)(2,1)S(1)}, u32[]{:S(2)}, u32[]{:S(2)}) collective-permute-start(bf16[256,256]{1,0:T(8,128)(2,1)S(1)} %pad_maximum_fusion.line_ref), channel_id=1, source_target_pairs={{0,6},{2,4},{4,2},{6,0},{8,14},{10,12},{12,10},{14,8},{16,22},{18,... | collective-permute-start | bytes 393224 | tf_op jit(solution)/shard_map/ppermute | solution.py:247
  13.8 0.5 %collective-permute-start.4 = (bf16[256,256]{1,0:T(8,128)(2,1)S(1)}, bf16[256,256]{1,0:T(8,128)(2,1)S(1)}, u32[]{:S(2)}, u32[]{:S(2)}) collective-permute-start(bf16[256,256]{1,0:T(8,128)(2,1)S(1)} %pad_maximum_fusion.line_ref), channel_id=1, source_target_pairs={{0,4},{2,6},{4,0},{6,2},{8,12},{10,14},{12,8},{14,10},{16,20},{18,... | collective-permute-start | bytes 393224 | tf_op jit(solution)/shard_map/ppermute | solution.py:247
  14.3 0.5 %collective-permute-start.3 = (bf16[256,256]{1,0:T(8,128)(2,1)S(1)}, bf16[256,256]{1,0:T(8,128)(2,1)S(1)}, u32[]{:S(2)}, u32[]{:S(2)}) collective-permute-start(bf16[256,256]{1,0:T(8,128)(2,1)S(1)} %pad_maximum_fusion.line_ref), channel_id=1, source_target_pairs={{0,2},{2,0},{4,6},{6,4},{8,10},{10,8},{12,14},{14,12},{16,18},{18,... | collective-permute-start | bytes 393224 | tf_op jit(solution)/shard_map/ppermute | solution.py:247
  14.8 0.9 %copy-done = bf16[128,1024]{1,0:T(8,128)(2,1)S(1)} copy-done((bf16[128,1024]{1,0:T(8,128)(2,1)S(1)}, bf16[128,1024]{1,0:T(8,128)(2,1)}, u32[]{:S(2)}) %copy-start) | copy-done | bytes 262168
  15.8 0.9 %copy-done.1 = bf16[128,1024]{1,0:T(8,128)(2,1)S(1)} copy-done((bf16[128,1024]{1,0:T(8,128)(2,1)S(1)}, bf16[128,1024]{1,0:T(8,128)(2,1)}, u32[]{:S(2)}) %copy-start.1) | copy-done | bytes 262168
  17.1 1.4 %collective-permute-done.5.refs_3_ = bf16[256,256]{1,0:T(8,128)(2,1)S(1)} collective-permute-done((bf16[256,256]{1,0:T(8,128)(2,1)S(1)}, bf16[256,256]{1,0:T(8,128)(2,1)S(1)}, u32[]{:S(2)}, u32[]{:S(2)}) %collective-permute-start.5) | collective-permute-done | bytes 131104 | tf_op jit(solution)/shard_map/ppermute | solution.py:247
  18.6 0.8 %collective-permute-done.4.refs_2_ = bf16[256,256]{1,0:T(8,128)(2,1)S(1)} collective-permute-done((bf16[256,256]{1,0:T(8,128)(2,1)S(1)}, bf16[256,256]{1,0:T(8,128)(2,1)S(1)}, u32[]{:S(2)}, u32[]{:S(2)}) %collective-permute-start.4) | collective-permute-done | bytes 131104 | tf_op jit(solution)/shard_map/ppermute | solution.py:247
  19.4 0.5 %collective-permute-start.7 = (bf16[256,256]{1,0:T(8,128)(2,1)S(1)}, bf16[256,256]{1,0:T(8,128)(2,1)S(1)}, u32[]{:S(2)}, u32[]{:S(2)}) collective-permute-start(bf16[256,256]{1,0:T(8,128)(2,1)S(1)} %collective-permute-done.3.refs_1_), channel_id=1, source_target_pairs={{0,1},{1,0},{2,3},{3,2},{4,5},{5,4},{6,7},{7,6},{8,9},{9,8},{10,11... | collective-permute-start | bytes 393224 | tf_op jit(solution)/shard_map/ppermute | solution.py:247
  19.9 0.8 %collective-permute-done.8.refs_6_ = bf16[256,256]{1,0:T(8,128)(2,1)S(1)} collective-permute-done((bf16[256,256]{1,0:T(8,128)(2,1)S(1)}, bf16[256,256]{1,0:T(8,128)(2,1)S(1)}, u32[]{:S(2)}, u32[]{:S(2)}) %collective-permute-start.8) | collective-permute-done | bytes 131104 | tf_op jit(solution)/shard_map/ppermute | solution.py:247
  20.9 0.7 %copy-done.2 = s32[8]{0:T(128)S(1)} copy-done((s32[8]{0:T(128)S(1)}, s32[8]{0:T(128)}, u32[]{:S(2)}) %copy-start.2) | copy-done | bytes 56
  21.6 2.5 %shard_map.77 = (bf16[2048,128]{1,0:T(8,128)(2,1)S(1)}, bf16[2,2048,512]{2,1,0:T(8,128)(2,1)S(1)}, bf16[256,256]{1,0:T(8,128)(2,1)S(1)}, bf16[256,256]{1,0:T(8,1...) custom-call(s32[8]{0:T(128)S(1)} %copy-done.2, ...), custom_call_target="tpu_custom_call" | custom-call | tf_op jit(solution)/shard_map/pallas_call | solution.py:209
  25.6 2.0 %collective-permute-start.16 = (bf16[256,256]{1,0:T(8,128)(2,1)S(1)}, bf16[256,256]{1,0:T(8,128)(2,1)S(1)}, u32[]{:S(2)}, u32[]{:S(2)}) collective-permute-start(bf16[256,256]{1,0:T(8,128)(2,1)S(1)} %add_convert_fusion.4.order_ref), channel_id=1, source_target_pairs={{0,6},{2,4},{4,2},{6,0},{8,14},{10,12},{12,10},{14,8},{16,22},{18,... | collective-permute-start | bytes 393224 | tf_op jit(solution)/shard_map/ppermute | solution.py:247
  27.6 1.5 %collective-permute-start.13 = (bf16[256,256]{1,0:T(8,128)(2,1)S(1)}, bf16[256,256]{1,0:T(8,128)(2,1)S(1)}, u32[]{:S(2)}, u32[]{:S(2)}) collective-permute-start(bf16[256,256]{1,0:T(8,128)(2,1)S(1)} %add_convert_fusion.2), channel_id=1, source_target_pairs={{0,2},{2,0},{4,6},{6,4},{8,10},{10,8},{12,14},{14,12},{16,18},{18,... | collective-permute-start | bytes 393224 | tf_op jit(solution)/shard_map/ppermute | solution.py:247
  29.3 3.5 %collective-permute-done.16 = bf16[256,256]{1,0:T(8,128)(2,1)S(1)} collective-permute-done((bf16[256,256]{1,0:T(8,128)(2,1)S(1)}, bf16[256,256]{1,0:T(8,128)(2,1)S(1)}, u32[]{:S(2)}, u32[]{:S(2)}) %collective-permute-start.16) | collective-permute-done | bytes 131104 | tf_op jit(solution)/shard_map/ppermute | solution.py:247
  32.9 2.5 %collective-permute-done.13 = bf16[256,256]{1,0:T(8,128)(2,1)S(1)} collective-permute-done((bf16[256,256]{1,0:T(8,128)(2,1)S(1)}, bf16[256,256]{1,0:T(8,128)(2,1)S(1)}, u32[]{:S(2)}, u32[]{:S(2)}) %collective-permute-start.13) | collective-permute-done | bytes 131104 | tf_op jit(solution)/shard_map/ppermute | solution.py:247
  35.7 6.0 %collective-permute-start.19 = (bf16[64,256]{1,0:T(8,128)(2,1)S(1)}, bf16[64,256]{1,0:T(8,128)(2,1)S(1)}, u32[]{:S(2)}, u32[]{:S(2)}) collective-permute-start(bf16[64,256]{1,0:T(8,128)(2,1)S(1)} %get-tuple-element.30), channel_id=1, source_target_pairs={{0,24},{2,26},{4,28},{6,30},{8,16},{10,18},{12,20},{14,22},{16,8},... | collective-permute-start | bytes 98312 | tf_op jit(solution)/shard_map/ppermute | solution.py:247
  42.2 1.9 %shard_map.78 = bf16[128,1024]{1,0:T(8,128)(2,1)} custom-call(s32[8]{0:T(128)S(1)} %copy-done.2, bf16[2048,128]{1,0:T(8,128)(2,1)S(1)} %get-tuple-element.19.keys_ref, bf16[2,2048,512]{2,1,0:T(8,128)(2,1)S(1)} %get-tuple-element.20.dlogits_ref, bf16[256,256]{1,0:T(8,128)(2,1)S(1)} %add_convert_fusion.4.order_ref), custom_call_target="tpu_custom_call" | custom-call | tf_op jit(solution)/shard_map/pallas_call | solution.py:233
  44.1 2.4 %collective-permute-done.18 = bf16[64,256]{1,0:T(8,128)(2,1)S(1)} collective-permute-done((bf16[64,256]{1,0:T(8,128)(2,1)S(1)}, bf16[64,256]{1,0:T(8,128)(2,1)S(1)}, u32[]{:S(2)}, u32[]{:S(2)}) %collective-permute-start.18) | collective-permute-done | bytes 32800 | tf_op jit(solution)/shard_map/ppermute | solution.py:247
  46.5 0.6 %fusion.2 = (bf16[64,128]{1,0:T(8,128)(2,1)}, bf16[64,128]{1,0:T(8,128)(2,1)}) fusion(bf16[64,256]{1,0:T(8,128)(2,1)S(1)} %add_convert_fusion.5), kind=kLoop, calls=%fused_computation.11 | loop fusion | bytes 65536 | tf_op jit(solution)/shard_map/slice | solution.py:294
  (34 shorter events, 3.2 us)
Async XLA Ops:
  1.4 6.9 %collective-permute-start.2 = (bf16[64,256]{1,0:T(8,128)(2,1)S(1)}, bf16[64,256]{1,0:T(8,128)(2,1)S(1)}, u32[]{:S(2)}, u32[]{:S(2)}) collective-permute-start(bf16[64,256]{1,0:T(8,128)(2,1)S(1)} %fusion), channel_id=1, source_target_pairs={{0,24},{2,26},{4,28},{6,30},{8,16},{10,18},{12,20},{14,22},{16,8},... | collective-permute-start | bytes 98312 | tf_op jit(solution)/shard_map/ppermute | solution.py:247
  6.4 4.8 %collective-permute-start.1 = (bf16[64,256]{1,0:T(8,128)(2,1)S(1)}, bf16[64,256]{1,0:T(8,128)(2,1)S(1)}, u32[]{:S(2)}, u32[]{:S(2)}) collective-permute-start(bf16[64,256]{1,0:T(8,128)(2,1)S(1)} %fusion), channel_id=1, source_target_pairs={{0,16},{2,18},{4,20},{6,22},{8,24},{10,26},{12,28},{14,30},{16,0},... | collective-permute-start | bytes 98312 | tf_op jit(solution)/shard_map/ppermute | solution.py:247
  6.4 4.8 %collective-permute-start = (bf16[64,256]{1,0:T(8,128)(2,1)S(1)}, bf16[64,256]{1,0:T(8,128)(2,1)S(1)}, u32[]{:S(2)}, u32[]{:S(2)}) collective-permute-start(bf16[64,256]{1,0:T(8,128)(2,1)S(1)} %fusion), channel_id=1, source_target_pairs={{0,8},{2,10},{4,12},{6,14},{8,0},{10,2},{12,4},{14,6},{16,24},{18,... | collective-permute-start | bytes 98312 | tf_op jit(solution)/shard_map/ppermute | solution.py:247
  11.3 7.3 %collective-permute-start.5 = (bf16[256,256]{1,0:T(8,128)(2,1)S(1)}, bf16[256,256]{1,0:T(8,128)(2,1)S(1)}, u32[]{:S(2)}, u32[]{:S(2)}) collective-permute-start(bf16[256,256]{1,0:T(8,128)(2,1)S(1)} %pad_maximum_fusion.line_ref), channel_id=1, source_target_pairs={{0,6},{2,4},{4,2},{6,0},{8,14},{10,12},{12,10},{14,8},{16,22},{18,... | collective-permute-start | bytes 393224 | tf_op jit(solution)/shard_map/ppermute | solution.py:247
  13.8 5.6 %collective-permute-start.4 = (bf16[256,256]{1,0:T(8,128)(2,1)S(1)}, bf16[256,256]{1,0:T(8,128)(2,1)S(1)}, u32[]{:S(2)}, u32[]{:S(2)}) collective-permute-start(bf16[256,256]{1,0:T(8,128)(2,1)S(1)} %pad_maximum_fusion.line_ref), channel_id=1, source_target_pairs={{0,4},{2,6},{4,0},{6,2},{8,12},{10,14},{12,8},{14,10},{16,20},{18,... | collective-permute-start | bytes 393224 | tf_op jit(solution)/shard_map/ppermute | solution.py:247
  14.3 5.1 %collective-permute-start.3 = (bf16[256,256]{1,0:T(8,128)(2,1)S(1)}, bf16[256,256]{1,0:T(8,128)(2,1)S(1)}, u32[]{:S(2)}, u32[]{:S(2)}) collective-permute-start(bf16[256,256]{1,0:T(8,128)(2,1)S(1)} %pad_maximum_fusion.line_ref), channel_id=1, source_target_pairs={{0,2},{2,0},{4,6},{6,4},{8,10},{10,8},{12,14},{14,12},{16,18},{18,... | collective-permute-start | bytes 393224 | tf_op jit(solution)/shard_map/ppermute | solution.py:247
  14.8 0.9 %copy-start = (bf16[128,1024]{1,0:T(8,128)(2,1)S(1)}, bf16[128,1024]{1,0:T(8,128)(2,1)}, u32[]{:S(2)}) copy-start(bf16[128,1024]{1,0:T(8,128)(2,1)} %q_hbm.1) | copy-start | bytes 786436
  15.8 0.9 %copy-start.1 = (bf16[128,1024]{1,0:T(8,128)(2,1)S(1)}, bf16[128,1024]{1,0:T(8,128)(2,1)}, u32[]{:S(2)}) copy-start(bf16[128,1024]{1,0:T(8,128)(2,1)} %g_hbm.1) | copy-start | bytes 786436
  17.1 2.8 %collective-permute-start.6 = (bf16[256,256]{1,0:T(8,128)(2,1)S(1)}, bf16[256,256]{1,0:T(8,128)(2,1)S(1)}, u32[]{:S(2)}, u32[]{:S(2)}) collective-permute-start(bf16[256,256]{1,0:T(8,128)(2,1)S(1)} %get-tuple-element.18.refs_0_), channel_id=1, source_target_pairs={{0,1},{1,0},{2,3},{3,2},{4,5},{5,4},{6,7},{7,6},{8,9},{9,8},{10,11... | collective-permute-start | bytes 393224 | tf_op jit(solution)/shard_map/ppermute | solution.py:247
  18.6 1.3 %collective-permute-start.9 = (bf16[256,256]{1,0:T(8,128)(2,1)S(1)}, bf16[256,256]{1,0:T(8,128)(2,1)S(1)}, u32[]{:S(2)}, u32[]{:S(2)}) collective-permute-start(bf16[256,256]{1,0:T(8,128)(2,1)S(1)} %collective-permute-done.5.refs_3_), channel_id=1, source_target_pairs={{0,1},{1,0},{2,3},{3,2},{4,5},{5,4},{6,7},{7,6},{8,9},{9,8},{10,11... | collective-permute-start | bytes 393224 | tf_op jit(solution)/shard_map/ppermute | solution.py:247
  19.4 1.3 %collective-permute-start.8 = (bf16[256,256]{1,0:T(8,128)(2,1)S(1)}, bf16[256,256]{1,0:T(8,128)(2,1)S(1)}, u32[]{:S(2)}, u32[]{:S(2)}) collective-permute-start(bf16[256,256]{1,0:T(8,128)(2,1)S(1)} %collective-permute-done.4.refs_2_), channel_id=1, source_target_pairs={{0,1},{1,0},{2,3},{3,2},{4,5},{5,4},{6,7},{7,6},{8,9},{9,8},{10,11... | collective-permute-start | bytes 393224 | tf_op jit(solution)/shard_map/ppermute | solution.py:247
  19.4 1.5 %collective-permute-start.7 = (bf16[256,256]{1,0:T(8,128)(2,1)S(1)}, bf16[256,256]{1,0:T(8,128)(2,1)S(1)}, u32[]{:S(2)}, u32[]{:S(2)}) collective-permute-start(bf16[256,256]{1,0:T(8,128)(2,1)S(1)} %collective-permute-done.3.refs_1_), channel_id=1, source_target_pairs={{0,1},{1,0},{2,3},{3,2},{4,5},{5,4},{6,7},{7,6},{8,9},{9,8},{10,11... | collective-permute-start | bytes 393224 | tf_op jit(solution)/shard_map/ppermute | solution.py:247
  20.9 0.7 %copy-start.2 = (s32[8]{0:T(128)S(1)}, s32[8]{0:T(128)}, u32[]{:S(2)}) copy-start(s32[8]{0:T(128)} %lengths_ref.3) | copy-start | bytes 100
  24.1 1.4 %collective-permute-start.10 = (bf16[256,256]{1,0:T(8,128)(2,1)S(1)}, bf16[256,256]{1,0:T(8,128)(2,1)S(1)}, u32[]{:S(2)}, u32[]{:S(2)}) collective-permute-start(bf16[256,256]{1,0:T(8,128)(2,1)S(1)} %get-tuple-element.22), channel_id=1, source_target_pairs={{0,1},{1,0},{2,3},{3,2},{4,5},{5,4},{6,7},{7,6},{8,9},{9,8},{10,11... | collective-permute-start | bytes 393224 | tf_op jit(solution)/shard_map/ppermute | solution.py:247
  24.5 4.8 %collective-permute-start.11 = (bf16[256,256]{1,0:T(8,128)(2,1)S(1)}, bf16[256,256]{1,0:T(8,128)(2,1)S(1)}, u32[]{:S(2)}, u32[]{:S(2)}) collective-permute-start(bf16[256,256]{1,0:T(8,128)(2,1)S(1)} %get-tuple-element.24), channel_id=1, source_target_pairs={{0,1},{1,0},{2,3},{3,2},{4,5},{5,4},{6,7},{7,6},{8,9},{9,8},{10,11... | collective-permute-start | bytes 393224 | tf_op jit(solution)/shard_map/ppermute | solution.py:247
  24.7 2.9 %collective-permute-start.12 = (bf16[256,256]{1,0:T(8,128)(2,1)S(1)}, bf16[256,256]{1,0:T(8,128)(2,1)S(1)}, u32[]{:S(2)}, u32[]{:S(2)}) collective-permute-start(bf16[256,256]{1,0:T(8,128)(2,1)S(1)} %get-tuple-element.26), channel_id=1, source_target_pairs={{0,1},{1,0},{2,3},{3,2},{4,5},{5,4},{6,7},{7,6},{8,9},{9,8},{10,11... | collective-permute-start | bytes 393224 | tf_op jit(solution)/shard_map/ppermute | solution.py:247
  25.0 4.1 %collective-permute-start.14 = (bf16[256,256]{1,0:T(8,128)(2,1)S(1)}, bf16[256,256]{1,0:T(8,128)(2,1)S(1)}, u32[]{:S(2)}, u32[]{:S(2)}) collective-permute-start(bf16[256,256]{1,0:T(8,128)(2,1)S(1)} %get-tuple-element.28), channel_id=1, source_target_pairs={{0,1},{1,0},{2,3},{3,2},{4,5},{5,4},{6,7},{7,6},{8,9},{9,8},{10,11... | collective-permute-start | bytes 393224 | tf_op jit(solution)/shard_map/ppermute | solution.py:247
  25.6 7.3 %collective-permute-start.16 = (bf16[256,256]{1,0:T(8,128)(2,1)S(1)}, bf16[256,256]{1,0:T(8,128)(2,1)S(1)}, u32[]{:S(2)}, u32[]{:S(2)}) collective-permute-start(bf16[256,256]{1,0:T(8,128)(2,1)S(1)} %add_convert_fusion.4.order_ref), channel_id=1, source_target_pairs={{0,6},{2,4},{4,2},{6,0},{8,14},{10,12},{12,10},{14,8},{16,22},{18,... | collective-permute-start | bytes 393224 | tf_op jit(solution)/shard_map/ppermute | solution.py:247
  27.6 7.7 %collective-permute-start.13 = (bf16[256,256]{1,0:T(8,128)(2,1)S(1)}, bf16[256,256]{1,0:T(8,128)(2,1)S(1)}, u32[]{:S(2)}, u32[]{:S(2)}) collective-permute-start(bf16[256,256]{1,0:T(8,128)(2,1)S(1)} %add_convert_fusion.2), channel_id=1, source_target_pairs={{0,2},{2,0},{4,6},{6,4},{8,10},{10,8},{12,14},{14,12},{16,18},{18,... | collective-permute-start | bytes 393224 | tf_op jit(solution)/shard_map/ppermute | solution.py:247
  29.2 6.2 %collective-permute-start.15 = (bf16[256,256]{1,0:T(8,128)(2,1)S(1)}, bf16[256,256]{1,0:T(8,128)(2,1)S(1)}, u32[]{:S(2)}, u32[]{:S(2)}) collective-permute-start(bf16[256,256]{1,0:T(8,128)(2,1)S(1)} %add_convert_fusion.1), channel_id=1, source_target_pairs={{0,4},{2,6},{4,0},{6,2},{8,12},{10,14},{12,8},{14,10},{16,20},{18,... | collective-permute-start | bytes 393224 | tf_op jit(solution)/shard_map/ppermute | solution.py:247
  35.5 8.6 %collective-permute-start.17 = (bf16[64,256]{1,0:T(8,128)(2,1)S(1)}, bf16[64,256]{1,0:T(8,128)(2,1)S(1)}, u32[]{:S(2)}, u32[]{:S(2)}) collective-permute-start(bf16[64,256]{1,0:T(8,128)(2,1)S(1)} %get-tuple-element.29), channel_id=1, source_target_pairs={{0,8},{2,10},{4,12},{6,14},{8,0},{10,2},{12,4},{14,6},{16,24},{18,... | collective-permute-start | bytes 98312 | tf_op jit(solution)/shard_map/ppermute | solution.py:247
  35.7 8.4 %collective-permute-start.19 = (bf16[64,256]{1,0:T(8,128)(2,1)S(1)}, bf16[64,256]{1,0:T(8,128)(2,1)S(1)}, u32[]{:S(2)}, u32[]{:S(2)}) collective-permute-start(bf16[64,256]{1,0:T(8,128)(2,1)S(1)} %get-tuple-element.30), channel_id=1, source_target_pairs={{0,24},{2,26},{4,28},{6,30},{8,16},{10,18},{12,20},{14,22},{16,8},... | collective-permute-start | bytes 98312 | tf_op jit(solution)/shard_map/ppermute | solution.py:247
  41.7 4.8 %collective-permute-start.18 = (bf16[64,256]{1,0:T(8,128)(2,1)S(1)}, bf16[64,256]{1,0:T(8,128)(2,1)S(1)}, u32[]{:S(2)}, u32[]{:S(2)}) collective-permute-start(bf16[64,256]{1,0:T(8,128)(2,1)S(1)} %get-tuple-element.31), channel_id=1, source_target_pairs={{0,16},{2,18},{4,20},{6,22},{8,24},{10,26},{12,28},{14,30},{16,0},... | collective-permute-start | bytes 98312 | tf_op jit(solution)/shard_map/ppermute | solution.py:247
